TPU v7x, 128 devices: a whole 4x4x4 slice. The times are simulated.
128 devices in a mesh: grid: 32 (over x, z, core), rep: 4 (over y).
Axes of the slice: x: 4, y: 4, z: 4, core: 2. Of those that a mesh axis runs over, the one named last changes fastest.
Arguments:
- density: bfloat16 [4096, 4096], P('grid', 'rep'), may hold values from -4.5 to 4.5
- pattern: int32 [32, 32], replicated, may hold values from 0 to 1, as said below
Outputs:
- sign_matrix: float32 [4096, 4096], P('grid', 'rep')
Inputs may be any that keep to these rules, and one draw needn't show every extreme that they name: `pattern`: Symmetric, with ones on the diagonal and beside it.
All inputs are finite; a program needn't handle non-finite values.
Results may differ from a plain program's by a relative error of at most 0.0035.
Values may be sent and summed in bfloat16 or wider, within the bound.
A program may use at most 64 MiB of HBM per device.

v0:
```python
import jax
import jax.numpy as jnp
from jax import lax
from jax.sharding import PartitionSpec as P

BLOCK = 128
STEPS = 2


def make_columns(left_tile, part_rows):
    return lax.dot_general(
        left_tile, part_rows, (((1,), (1,)), ((), ())), preferred_element_type=jnp.float32
    )


def per_device(density, pattern):
    tile_rows, tile_cols = density.shape
    replicas = lax.axis_size("rep")
    order = tile_cols * replicas
    slab_blocks = tile_rows // BLOCK
    grid_pos = lax.axis_index("grid")
    rep_pos = lax.axis_index("rep")
    slab_pattern = lax.dynamic_slice_in_dim(pattern, grid_pos * slab_blocks, slab_blocks, 0)
    slab_keep = jnp.repeat(jnp.repeat(slab_pattern, BLOCK, axis=0), BLOCK, axis=1) > 0
    tile_keep = lax.dynamic_slice_in_dim(slab_keep, rep_pos * tile_cols, tile_cols, 1)
    state_tile = jnp.where(tile_keep, density, jnp.zeros_like(density))

    def product(left_tile, right_tile):
        partial_terms = make_columns(
            left_tile, lax.all_gather(right_tile, "grid", axis=0, tiled=True)
        )
        return lax.psum_scatter(partial_terms, "rep", scatter_dimension=1, tiled=True)

    state = state_tile
    for iteration in range(STEPS):
        square = jnp.where(tile_keep, product(state, state) / order, jnp.float32(0.0)).astype(
            jnp.bfloat16
        )
        cubic = product(state, square)
        updated = jnp.where(
            tile_keep, 1.5 * state.astype(jnp.float32) - 0.5 * cubic, jnp.float32(0.0)
        )
        if iteration + 1 < STEPS:
            state = updated.astype(jnp.bfloat16)
        else:
            state = updated
    return state


def solution(mesh):
    placed = (P("grid", "rep"), P())
    return jax.shard_map(
        per_device, mesh=mesh, in_specs=placed, out_specs=P("grid", "rep"), check_vma=False
    )
```

profile of v0, /device:TPU:1, one launch (start us, length us, event | category | flops | bytes accessed | tf_op | source)
XLA Modules:
  0.0 388.3 jit_solution(14354770601605882190)
XLA Ops:
  6.5 0.7 compare_bitcast_fusion
  7.2 0.1 broadcast_bitcast_fusion
  7.3 1.7 broadcast_select_fusion
  9.0 0.0 reduce-scatter.5.cloned.1.call-start
  9.1 57.2 %all-gather.5.cloned.1.call-done = bf16[4096,1024]{1,0:T(8,128)(2,1)} async-done(((bf16[128,1024]{1,0:T(8,128)(2,1)}), bf16[4096,1024]{1,0:T(8,128)(2,1)}) %all-gather.5.cloned.1.call-update) | async-done | bytes 8388624 | tf_op jit(solution)/shard_map/all_gather | solution.py:30
  66.3 7.7 %fusion = f32[128,4096]{1,0:T(8,128)} fusion(bf16[128,1024]{1,0:T(8,128)(2,1)} %broadcast_select_fusion, bf16[4096,1024]{1,0:T(8,128)(2,1)} %all-gather.5.cloned.1.call-done), kind=kOutput, calls=%fused_computation.7 | convolution fusion | flops 1073741824 | bytes 10747904 | tf_op jit(solution)/shard_map/dot_general | solution.py:11
  74.0 0.0 all-gather.7.cloned.1.call-start
  74.1 28.9 %reduce-scatter.5.cloned.1.call-done = f32[128,1024]{1,0:T(8,128)} async-done(((f32[128,4096]{1,0:T(8,128)}), f32[128,1024]{1,0:T(8,128)}) %reduce-scatter.5.cloned.1.call-update) | async-done | bytes 524304 | tf_op jit(solution)/shard_map/reduce_scatter | solution.py:32
  103.0 1.8 select_convert_fusion.2
  104.9 53.8 %all-gather.7.cloned.1.call-done = bf16[4096,1024]{1,0:T(8,128)(2,1)} async-done(((bf16[128,1024]{1,0:T(8,128)(2,1)}), bf16[4096,1024]{1,0:T(8,128)(2,1)}) %all-gather.7.cloned.1.call-update) | async-done | bytes 8388624 | tf_op jit(solution)/shard_map/all_gather | solution.py:30
  158.7 7.6 %fusion.1 = f32[128,4096]{1,0:T(8,128)} fusion(bf16[128,1024]{1,0:T(8,128)(2,1)S(1)} %copy-done.1, bf16[4096,1024]{1,0:T(8,128)(2,1)} %all-gather.7.cloned.1.call-done), kind=kOutput, calls=%fused_computation.8 | convolution fusion | flops 1073741824 | bytes 10747904 | tf_op jit(solution)/shard_map/dot_general | solution.py:11
  166.3 0.0 all-gather.9.cloned.1.call-start
  166.4 28.9 %reduce-scatter.7.cloned.1.call-done = f32[128,1024]{1,0:T(8,128)} async-done(((f32[128,4096]{1,0:T(8,128)}), f32[128,1024]{1,0:T(8,128)}) %reduce-scatter.7.cloned.1.call-update) | async-done | bytes 524304 | tf_op jit(solution)/shard_map/reduce_scatter | solution.py:32
  195.3 1.9 select_convert_fusion.1
  197.2 0.0 reduce-scatter.9.cloned.1.call-start
  197.2 53.3 %all-gather.9.cloned.1.call-done = bf16[4096,1024]{1,0:T(8,128)(2,1)} async-done(((bf16[128,1024]{1,0:T(8,128)(2,1)}), bf16[4096,1024]{1,0:T(8,128)(2,1)}) %all-gather.9.cloned.1.call-update) | async-done | bytes 8388624 | tf_op jit(solution)/shard_map/all_gather | solution.py:30
  250.5 7.7 %fusion.2 = f32[128,4096]{1,0:T(8,128)} fusion(bf16[128,1024]{1,0:T(8,128)(2,1)} %select_convert_fusion.1, bf16[4096,1024]{1,0:T(8,128)(2,1)} %all-gather.9.cloned.1.call-done), kind=kOutput, calls=%fused_computation.9 | convolution fusion | flops 1073741824 | bytes 10747904 | tf_op jit(solution)/shard_map/dot_general | solution.py:11
  258.3 0.0 all-gather.11.cloned.1.call-start
  258.3 28.9 %reduce-scatter.9.cloned.1.call-done = f32[128,1024]{1,0:T(8,128)} async-done(((f32[128,4096]{1,0:T(8,128)}), f32[128,1024]{1,0:T(8,128)}) %reduce-scatter.9.cloned.1.call-update) | async-done | bytes 524304 | tf_op jit(solution)/shard_map/reduce_scatter | solution.py:32
  287.2 1.8 select_convert_fusion
  289.1 53.8 %all-gather.11.cloned.1.call-done = bf16[4096,1024]{1,0:T(8,128)(2,1)} async-done(((bf16[128,1024]{1,0:T(8,128)(2,1)}), bf16[4096,1024]{1,0:T(8,128)(2,1)}) %all-gather.11.cloned.1.call-update) | async-done | bytes 8388624 | tf_op jit(solution)/shard_map/all_gather | solution.py:30
  342.9 7.6 %fusion.3 = f32[128,4096]{1,0:T(8,128)} fusion(bf16[128,1024]{1,0:T(8,128)(2,1)S(1)} %copy-done, bf16[4096,1024]{1,0:T(8,128)(2,1)} %all-gather.11.cloned.1.call-done), kind=kOutput, calls=%fused_computation.10 | convolution fusion | flops 1073741824 | bytes 10747904 | tf_op jit(solution)/shard_map/dot_general | solution.py:11
  350.5 29.0 %reduce-scatter.11.cloned.1.call-done = f32[128,1024]{1,0:T(8,128)} async-done(((f32[128,4096]{1,0:T(8,128)}), f32[128,1024]{1,0:T(8,128)}) %reduce-scatter.11.cloned.1.call-update) | async-done | bytes 524304 | tf_op jit(solution)/shard_map/reduce_scatter | solution.py:32
  379.5 1.9 subtract_select_fusion
  (18 shorter events, 0.2 us)
Async XLA Ops:
  6.5 59.8 %all-gather.5.cloned.1.call-start = ((), (), s32[]{:S(2)}) async-start(), calls=%async_computation.4 | async-start | bytes 8650752 | tf_op jit(solution)/shard_map/all_gather | solution.py:30
  9.0 149.7 %copy-start.1 = (bf16[128,1024]{1,0:T(8,128)(2,1)S(1)}, bf16[128,1024]{1,0:T(8,128)(2,1)}, u32[]{:S(2)}) copy-start(bf16[128,1024]{1,0:T(8,128)(2,1)} %broadcast_select_fusion) | copy-start | bytes 786436
  9.0 94.0 %reduce-scatter.5.cloned.1.call-start = ((), (), s32[]{:S(2)}) async-start(), calls=%async_computation.5 | async-start | bytes 2621440 | tf_op jit(solution)/shard_map/reduce_scatter | solution.py:32
  74.0 121.3 %copy-start.2 = (bf16[128,1024]{1,0:T(8,128)(2,1)S(1)}, bf16[128,1024]{1,0:T(8,128)(2,1)}, u32[]{:S(2)}) copy-start(bf16[128,1024]{1,0:T(8,128)(2,1)} %param.2) | copy-start | bytes 786436
  74.0 84.6 %all-gather.7.cloned.1.call-start = ((), (), s32[]{:S(2)}) async-start(), calls=%async_computation.6 | async-start | bytes 8650752 | tf_op jit(solution)/shard_map/all_gather | solution.py:30
  104.8 90.5 %reduce-scatter.7.cloned.1.call-start = ((), (), s32[]{:S(2)}) async-start(), calls=%async_computation.7 | async-start | bytes 2621440 | tf_op jit(solution)/shard_map/reduce_scatter | solution.py:32
  166.3 84.2 %all-gather.9.cloned.1.call-start = ((), (), s32[]{:S(2)}) async-start(), calls=%async_computation.8 | async-start | bytes 8650752 | tf_op jit(solution)/shard_map/all_gather | solution.py:30
  197.2 145.7 %copy-start = (bf16[128,1024]{1,0:T(8,128)(2,1)S(1)}, bf16[128,1024]{1,0:T(8,128)(2,1)}, u32[]{:S(2)}) copy-start(bf16[128,1024]{1,0:T(8,128)(2,1)} %select_convert_fusion.1) | copy-start | bytes 786436
  197.2 90.0 %reduce-scatter.9.cloned.1.call-start = ((), (), s32[]{:S(2)}) async-start(), calls=%async_computation.9 | async-start | bytes 2621440 | tf_op jit(solution)/shard_map/reduce_scatter | solution.py:32
  258.3 84.6 %all-gather.11.cloned.1.call-start = ((), (), s32[]{:S(2)}) async-start(), calls=%async_computation.10 | async-start | bytes 8650752 | tf_op jit(solution)/shard_map/all_gather | solution.py:30
  289.1 90.4 %reduce-scatter.11.cloned.1.call-start = ((), (), s32[]{:S(2)}) async-start(), calls=%async_computation.11 | async-start | bytes 2621440 | tf_op jit(solution)/shard_map/reduce_scatter | solution.py:32
Sparse Core Ops, SparseCore 0:
  9.6 56.6 all-gather.4
  74.2 28.8 reduce-scatter.4
  105.5 53.0 all-gather.6
  166.4 28.8 reduce-scatter.6
  197.4 53.0 all-gather.8
  258.4 28.8 reduce-scatter.8
  289.8 53.0 all-gather.10
  350.7 28.7 reduce-scatter.10
where the time goes:
time: 389 us; the launch traced here: 388 us
  waiting for transfers between devices  334 us (86%)
  matrix products  30.6 us (8%)
  between operations  13.5 us (3%)
  other arithmetic  9.76 us (3%)
    all_gather x4, waiting for transfers between devices, product(): lax.all_gather(right_tile, 'grid', axis=0, tiled=True)  218 us
    reduce_scatter x4, waiting for transfers between devices, product(): lax.psum_scatter(partial_terms, 'rep', scatter_dimension=1, tiled=True)  116 us
    dot_general x4, matrix products, make_columns(): lax.dot_general(left_tile, part_rows, (((1,), (1,)), ((), ())), preferred...  30.6 us
  transfers between devices with their start and end apart: 8, of which 8 were waited for; matrix products, arithmetic and copies ran while one was open for 0% of the time, Pallas kernels for 0%

commit v1 on v0

v1 whole, which is shorter than its diff:
```python
import jax
import jax.numpy as jnp
from jax import lax
from jax.experimental import pallas as pl
from jax.experimental.pallas import tpu as pltpu
from jax.sharding import PartitionSpec as P

BLOCK = 128
STEPS = 2
ORDER = 4096
MESH = pl.DeviceIdType.MESH
RING = 4
PAIR = 2 * BLOCK
FAR_FIRST = (2, 1, 3)
NEAR_FIRST = (1, 3, 2)

GATHER_I = 0
GATHER_J = 3
SIBLING = 6
REDUCE_Q = 10
GATHER_Q = 22
REDUCE_C = 34
RELAY = 46
TURNED = 49
HAND_OVER = 52
SLOTS = 56


def nt_dot(left, right):
    return lax.dot_general(left, right, (((1,), (1,)), ((), ())), preferred_element_type=jnp.float32)


def block_of(outer, z, core):
    return outer * 8 + z * 2 + core


def kernel(density, pattern, out, rows_i, rows_j, send_q, got_q, own_q, square, send_c, got_c, own_c,
           unit, relay, turned, final, got_final, send_sem, recv_sem):
    grid_pos = lax.axis_index("grid")
    y = lax.axis_index("rep")
    x = grid_pos // 8
    z = (grid_pos // 2) % 4
    core = grid_pos % 2

    def device(step, p, q, z_at, core_at):
        x_at, y_at = (p, q) if step == 0 else (q, p)
        return ((x_at * 4 + z_at) * 2 + core_at, y_at)

    def copy(src, dst, step, slot, target):
        at = step * SLOTS + slot
        return pltpu.make_async_remote_copy(
            src_ref=src, dst_ref=dst, send_sem=send_sem.at[at], recv_sem=recv_sem.at[at],
            device_id=target, device_id_type=MESH,
        )

    def rows(start, size):
        return pl.ds(pl.multiple_of(start, size), size)

    def turn(a, d):
        return (a + d) % RING

    barrier = pltpu.get_barrier_semaphore()
    partners = [device(0, x, y, z, 1 - core)]
    for d in (1, 2, 3):
        partners += [device(0, turn(x, d), y, z, core), device(0, x, turn(y, d), z, core),
                     device(0, x, y, turn(z, d), core)]
    for partner in partners:
        pl.semaphore_signal(barrier, inc=1, device_id=partner, device_id_type=MESH)

    def keep(row_block, col_block):
        return pattern[row_block, col_block].astype(jnp.float32)

    mine = rows(x * PAIR + core * BLOCK, BLOCK)
    for b in range(8):
        cols = pl.ds(b * BLOCK, BLOCK)
        masked = density[:, cols].astype(jnp.float32) * keep(block_of(x, z, core), y * 8 + b)
        rows_j[0, mine, cols] = masked.astype(jnp.bfloat16)
    pl.semaphore_wait(barrier, len(partners))

    sends = []

    def start(c):
        c.start()
        sends.append(c)

    for step in range(STEPS):
        p, q = (x, y) if step == 0 else (y, x)
        here = device(step, p, q, z, core)
        sibling = device(step, p, q, z, 1 - core)
        own = rows(p * PAIR + core * BLOCK, BLOCK)
        own_src = rows_j.at[step, own]

        def arrival(dst, slot, step=step, here=here):
            return copy(dst, dst, step, slot, here)

        for d in NEAR_FIRST:
            start(copy(own_src, rows_j.at[step, own], step, GATHER_J + d - 1, device(step, turn(p, d), q, z, core)))
            start(copy(own_src, rows_i.at[step, rows(z * BLOCK, BLOCK)], step, GATHER_I + d - 1,
                       device(step, p, q, turn(z, d), core)))
        if step == 0:
            start(copy(own_src, own_src, step, SIBLING, sibling))
        rows_i[step, rows(z * BLOCK, BLOCK), :] = rows_j[step, own, :]
        if step == 0:
            arrival(rows_j.at[step, rows(p * PAIR + (1 - core) * BLOCK, BLOCK)], SIBLING).wait_recv()
            for b in range(4):
                unit[0, :, pl.ds(b * BLOCK, BLOCK)] = rows_j[0, rows(p * PAIR, PAIR), rows((2 * b + core) * BLOCK, BLOCK)]
        lag = turn(p - q, RING)

        @pl.when(lag != 0)
        def _(step=step, p=p, q=q, lag=lag):
            copy(unit.at[step], relay.at[step, lag - 1], step, RELAY + lag - 1, device(step, p, p, z, core)).start()

        for d in NEAR_FIRST:
            there = rows_j.at[step, rows(turn(p, RING - d) * PAIR + core * BLOCK, BLOCK)]
            arrival(there, GATHER_J + d - 1).wait_recv()
            start(copy(there, there, step, SIBLING + d, sibling))
        for d in NEAR_FIRST:
            arrival(rows_i.at[step, rows(turn(z, RING - d) * BLOCK, BLOCK)], GATHER_I + d - 1).wait_recv()
        for d in NEAR_FIRST:
            arrival(rows_j.at[step, rows(turn(p, RING - d) * PAIR + (1 - core) * BLOCK, BLOCK)], SIBLING + d).wait_recv()

        for half in range(2):
            lines = pl.ds(half * PAIR, PAIR)
            left = rows_i[step, lines, :]
            for d in FAR_FIRST:
                send_q[step, d - 1, lines, :] = nt_dot(left, rows_j[step, rows(turn(q, d) * PAIR, PAIR), :]).astype(jnp.bfloat16)
            for chunk in (2 * half, 2 * half + 1):
                part = pl.ds(chunk * BLOCK, BLOCK)
                for d in FAR_FIRST:
                    start(copy(send_q.at[step, d - 1, part], got_q.at[step, d - 1, part], step,
                               REDUCE_Q + 3 * chunk + d - 1, device(step, p, turn(q, d), z, core)))
            own_q[lines, :] = nt_dot(left, rows_j[step, rows(q * PAIR, PAIR), :])

        @pl.when(lag == 0)
        def _(step=step, p=p, q=q, here=here):
            for d in (1, 2, 3):
                copy(relay.at[step, d - 1], relay.at[step, d - 1], step, RELAY + d - 1, here).wait_recv()
                copy(relay.at[step, d - 1], turned.at[step], step, TURNED + d - 1, device(step, turn(p, RING - d), q, z, core)).start()
            turned[step] = unit[step]

        def add_square(chunk, step=step, p=p, q=q):
            part = pl.ds(chunk * BLOCK, BLOCK)
            total = own_q[part, :]
            for d in FAR_FIRST:
                arrival(got_q.at[step, d - 1, part], REDUCE_Q + 3 * chunk + d - 1).wait_recv()
                total += got_q[step, d - 1, part, :].astype(jnp.float32)
            for b in range(2):
                scale = keep(block_of(p, chunk, core), block_of(q, z, b)) * (1.0 / ORDER)
                square[step, part, rows(z * PAIR + b * BLOCK, BLOCK)] = (
                    total[:, b * BLOCK:(b + 1) * BLOCK] * scale).astype(jnp.bfloat16)
            block = square.at[step, part, rows(z * PAIR, PAIR)]
            for d in NEAR_FIRST:
                start(copy(block, block, step, GATHER_Q + 3 * chunk + d - 1, device(step, p, q, turn(z, d), core)))

        def cubic_terms(chunk, step=step, p=p, q=q):
            part = pl.ds(chunk * BLOCK, BLOCK)
            for d in NEAR_FIRST:
                arrival(square.at[step, part, rows(turn(z, RING - d) * PAIR, PAIR)], GATHER_Q + 3 * chunk + d - 1).wait_recv()
            right = square[step, part, :]
            for d in FAR_FIRST:
                send_c[step, d - 1, chunk] = nt_dot(rows_j[step, rows(turn(q, d) * PAIR, PAIR), :], right).astype(jnp.bfloat16)
                start(copy(send_c.at[step, d - 1, chunk], got_c.at[step, d - 1, chunk], step,
                           REDUCE_C + 3 * chunk + d - 1, device(step, p, turn(q, d), z, core)))
            own_c[chunk] = nt_dot(rows_j[step, rows(q * PAIR, PAIR), :], right)

        def add_cubic(chunk, step=step, p=p, q=q, sibling=sibling):
            total = own_c[chunk]
            for d in FAR_FIRST:
                arrival(got_c.at[step, d - 1, chunk], REDUCE_C + 3 * chunk + d - 1).wait_recv()
                total += got_c[step, d - 1, chunk].astype(jnp.float32)
            updated = 1.5 * turned[step, :, pl.ds(chunk * BLOCK, BLOCK)].astype(jnp.float32) - 0.5 * total
            halves = [updated[b * BLOCK:(b + 1) * BLOCK] * keep(block_of(q, z, b), block_of(p, chunk, core)) for b in range(2)]
            if step + 1 < STEPS:
                cols = pl.ds(chunk * BLOCK, BLOCK)
                for b in range(2):
                    unit[step + 1, pl.ds(b * BLOCK, BLOCK), cols] = halves[b].astype(jnp.bfloat16)
                place = rows_j.at[step + 1, rows(q * PAIR, PAIR), rows((2 * chunk + core) * BLOCK, BLOCK)]
                place[...] = unit[step + 1, :, cols]
                start(copy(place, place, step, HAND_OVER + chunk, sibling))
            else:
                for b in range(2):
                    final[chunk, pl.ds(b * BLOCK, BLOCK), :] = halves[b]
                out[:, rows((2 * chunk + core) * BLOCK, BLOCK)] = final[chunk, rows(core * BLOCK, BLOCK), :]
                start(copy(final.at[chunk, rows((1 - core) * BLOCK, BLOCK)], got_final.at[chunk], step,
                           HAND_OVER + chunk, sibling))

        add_square(0)
        add_square(1)
        add_square(2)
        cubic_terms(0)
        add_square(3)
        cubic_terms(1)
        cubic_terms(2)

        @pl.when(lag != 0)
        def _(step=step, here=here, lag=lag):
            copy(turned.at[step], turned.at[step], step, TURNED + RING - lag - 1, here).wait_recv()

        add_cubic(0)
        cubic_terms(3)
        add_cubic(1)
        add_cubic(2)
        add_cubic(3)
        for chunk in range(4):
            cols = rows((2 * chunk + 1 - core) * BLOCK, BLOCK)
            if step + 1 < STEPS:
                arrival(rows_j.at[step + 1, rows(q * PAIR, PAIR), cols], HAND_OVER + chunk).wait_recv()
            else:
                arrival(got_final.at[chunk], HAND_OVER + chunk).wait_recv()
                out[:, cols] = got_final[chunk]

    for c in sends:
        c.wait_send()
    for step in range(STEPS):
        p, q = (x, y) if step == 0 else (y, x)
        lag = turn(p - q, RING)

        @pl.when(lag != 0)
        def _(step=step, p=p, q=q, lag=lag):
            copy(unit.at[step], relay.at[step, lag - 1], step, RELAY + lag - 1, device(step, p, p, z, core)).wait_send()

        @pl.when(lag == 0)
        def _(step=step, p=p, q=q):
            for d in (1, 2, 3):
                copy(relay.at[step, d - 1], turned.at[step], step, TURNED + d - 1, device(step, turn(p, RING - d), q, z, core)).wait_send()


def per_device(density, pattern):
    bf16, f32 = jnp.bfloat16, jnp.float32
    quarter = ORDER // RING
    return pl.pallas_call(
        kernel,
        out_shape=jax.ShapeDtypeStruct(density.shape, f32),
        in_specs=[pl.BlockSpec(memory_space=pltpu.VMEM), pl.BlockSpec(memory_space=pltpu.SMEM)],
        out_specs=pl.BlockSpec(memory_space=pltpu.VMEM),
        scratch_shapes=[
            pltpu.VMEM((STEPS, 4 * BLOCK, quarter), bf16),
            pltpu.VMEM((STEPS, 8 * BLOCK, quarter), bf16),
            pltpu.VMEM((STEPS, 3, 4 * BLOCK, PAIR), bf16),
            pltpu.VMEM((STEPS, 3, 4 * BLOCK, PAIR), bf16),
            pltpu.VMEM((4 * BLOCK, PAIR), f32),
            pltpu.VMEM((STEPS, 4 * BLOCK, quarter), bf16),
            pltpu.VMEM((STEPS, 3, 4, PAIR, BLOCK), bf16),
            pltpu.VMEM((STEPS, 3, 4, PAIR, BLOCK), bf16),
            pltpu.VMEM((4, PAIR, BLOCK), f32),
            pltpu.VMEM((STEPS, PAIR, 4 * BLOCK), bf16),
            pltpu.VMEM((STEPS, 3, PAIR, 4 * BLOCK), bf16),
            pltpu.VMEM((STEPS, PAIR, 4 * BLOCK), bf16),
            pltpu.VMEM((4, PAIR, BLOCK), f32),
            pltpu.VMEM((4, BLOCK, BLOCK), f32),
            pltpu.SemaphoreType.DMA((STEPS * SLOTS,)),
            pltpu.SemaphoreType.DMA((STEPS * SLOTS,)),
        ],
        compiler_params=pltpu.CompilerParams(
            collective_id=0, has_side_effects=True, vmem_limit_bytes=56 * 2**20
        ),
        name="polar_steps",
    )(density, pattern)


def solution(mesh):
    placed = (P("grid", "rep"), P())
    return jax.shard_map(
        per_device, mesh=mesh, in_specs=placed, out_specs=P("grid", "rep"), check_vma=False
    )
```

time: 389 us -> 98.2 us (0.25)
  waiting for transfers between devices: 334 us -> 0 us
  Pallas kernels: 0 us -> 96.1 us
  matrix products: 30.6 us -> 0 us
  between operations: 13.5 us -> 0.01 us
  other arithmetic: 9.76 us -> 0 us
    all_gather x4 -> x0, waiting for transfers between devices: 218 us -> none  [product(): lax.all_gather(right_tile, 'grid', axis=0, tiled=True)]
    reduce_scatter x4 -> x0, waiting for transfers between devices: 116 us -> none  [product(): lax.psum_scatter(partial_terms, 'rep', scatter_dimension=1, tiled=True)]
    pallas_call x0 -> x1, Pallas kernels: none -> 96.1 us  [per_device(): pl.pallas_call(kernel, out_shape=jax.ShapeDtypeStruct(density.shape, f32)...]
    dot_general x4 -> x0, matrix products: 30.6 us -> none  [make_columns(): lax.dot_general(left_tile, part_rows, (((1,), (1,)), ((), ())), preferred...]
    convert_element_type x3 -> x0, other arithmetic: 5.46 us -> none  [the longest x2 3.6 us: per_device(): jnp.where(tile_keep, product(state, state) / order, jnp.float32(0.0))]
  transfers between devices with their start and end apart: 8 -> 0, of which waited for: 8 -> 0; matrix products, arithmetic and copies ran while one was open for 0% -> 0% of each run, Pallas kernels for 0% -> 0%
where the time goes in v1:
time: 98.2 us; the launch traced here: 98 us
  Pallas kernels  96.1 us (98%)
  local copies, waits for them, and re-layouts  1.89 us (2%)
    pallas_call x1, Pallas kernels, per_device(): pl.pallas_call(kernel, out_shape=jax.ShapeDtypeStruct(density.shape, f32)...  96.1 us

profile of v1, /device:TPU:1, one launch (start us, length us, event | category | flops | bytes accessed | tf_op | source)
XLA Modules:
  0.0 98.0 jit_solution(8570401776909119883)
XLA Ops:
  0.0 96.1 %polar_steps.1 = f32[128,1024]{1,0:T(8,128)} custom-call(bf16[128,1024]{1,0:T(8,128)(2,1)} %density.1, s32[32,32]{1,0:T(8,128)} %pattern.1), custom_call_target="tpu_custom_call" | custom-call | tf_op jit(solution)/shard_map/polar_steps/pallas_call | solution.py:231
  96.1 1.9 %copy.4 = f32[128,1024]{1,0:T(8,128)} copy(f32[128,1024]{1,0:T(8,128)} %polar_steps.1) | data formatting | bytes 1048576

commit v2 on v0

v2 whole, which is shorter than its diff:
```python
import math

import jax
import jax.numpy as jnp
from jax import lax
from jax.experimental import pallas as pl
from jax.experimental.pallas import tpu as pltpu
from jax.sharding import PartitionSpec as P

BLOCK = 128
STEPS = 2
ORDER = 4096
MESH = pl.DeviceIdType.MESH
RING = 4
PAIR = 2 * BLOCK
HALF = BLOCK // 2
FAR_FIRST = (2, 1, 3)
NEAR_FIRST = (1, 3, 2)

GROUPS = ("first", "second", "step 1", "step 2", "relay", "relay again")
STEP_GROUPS = GROUPS[2:4]
ARRIVALS = 48


def nt_dot(left, right):
    return lax.dot_general(left, right, (((1,), (1,)), ((), ())), preferred_element_type=jnp.float32)


def block_of(outer, z, core):
    return outer * 8 + z * 2 + core


def kernel(density, pattern_in, out, loaded, pattern, rows_i, rows_j, send_q, got_q, own_q, square, send_c, got_c, own_c,
           unit, relay, turned, final, load_sem, store_sem, send_sem, recv_sem):
    grid_pos = lax.axis_index("grid")
    y = lax.axis_index("rep")
    x = grid_pos // 8
    z = (grid_pos // 2) % 4
    core = grid_pos % 2
    other = 1 - core

    def device(step, p, q, z_at, core_at):
        x_at, y_at = (p, q) if step == 0 else (q, p)
        return ((x_at * 4 + z_at) * 2 + core_at, y_at)

    slots = {}
    groups = {}

    def slot(*key):
        return slots.setdefault(key, len(slots))

    def copy_at(src, dst, group, at, target):
        return pltpu.make_async_remote_copy(
            src_ref=src, dst_ref=dst, send_sem=send_sem.at[group], recv_sem=recv_sem.at[at],
            device_id=target, device_id_type=MESH,
        )

    def rows(start, size):
        return pl.ds(pl.multiple_of(start, size), size)

    def turn(a, d):
        return (a + d) % RING

    barrier = pltpu.get_barrier_semaphore()
    partners = [device(0, x, y, z, other)]
    for d in (1, 2, 3):
        partners += [device(0, turn(x, d), y, z, core), device(0, x, turn(y, d), z, core),
                     device(0, x, y, turn(z, d), core), device(0, x, y, turn(z, d), other)]
    for partner in partners:
        pl.semaphore_signal(barrier, inc=1, device_id=partner, device_id_type=MESH)
    loads = [pltpu.make_async_copy(density, loaded, load_sem.at[0]), pltpu.make_async_copy(pattern_in, pattern, load_sem.at[1])]
    for load in loads:
        load.start()
    for load in loads:
        load.wait()

    def keep(row_block, col_block):
        return pattern[row_block, col_block].astype(jnp.float32)

    mine = rows(x * PAIR + core * BLOCK, BLOCK)
    for b in range(8):
        cols = pl.ds(b * BLOCK, BLOCK)
        masked = loaded[:, cols].astype(jnp.float32) * keep(block_of(x, z, core), y * 8 + b)
        rows_j[0, mine, cols] = masked.astype(jnp.bfloat16)
    pl.semaphore_wait(barrier, len(partners))

    stores = []

    def total(size):
        return rows_j.at[:, pl.ds(0, size // (2 * STEPS * rows_j.shape[2]))]

    def bytes_of(ref):
        return math.prod(ref.shape) * jnp.dtype(ref.dtype).itemsize

    def send(src, dst, target, group, *key):
        copy_at(src, dst, GROUPS.index(group), slot(*key), target).start()
        groups[group] = groups.get(group, 0) + bytes_of(src)

    def await_copy(dst, *key):
        copy_at(dst, dst, 0, slot(*key), (grid_pos, y)).wait_recv()

    def gather_first(p, q):
        sibling = device(0, p, q, z, other)

        def target(ring, d):
            return device(0, turn(p, d), q, z, core) if ring == "j" else device(0, p, q, turn(z, d), core)

        def place(ring, d, half, core_at=core):
            if ring == "j":
                return rows_j.at[0, rows(turn(p, d) * PAIR + core_at * BLOCK + half * HALF, HALF)]
            return rows_i.at[0, rows(turn(z, d) * BLOCK + half * HALF, HALF)]

        own = [rows_j.at[0, rows(p * PAIR + core * BLOCK + half * HALF, HALF)] for half in range(2)]
        for d, half in ((1, 0), (3, 1)):
            send(own[half], place("j", 0, half), target("j", d), "first", "near", "j", d)
            send(own[half], place("i", 0, half), target("i", d), "first", "near", "i", d)
        whole = rows_j.at[0, rows(p * PAIR + core * BLOCK, BLOCK)]
        send(whole, whole, sibling, "first", "pair")
        for d, half in ((1, 1), (3, 0)):
            send(own[half], place("j", 0, half), target("j", d), "first", "late", "j")
            send(own[half], place("i", 0, half), target("i", d), "first", "late", "i")
        rows_i[0, rows(z * BLOCK, BLOCK), :] = rows_j[0, rows(p * PAIR + core * BLOCK, BLOCK), :]
        await_copy(rows_j.at[0, rows(p * PAIR + other * BLOCK, BLOCK)], "pair")
        for b in range(4):
            unit[0, :, pl.ds(b * BLOCK, BLOCK)] = rows_j[0, rows(p * PAIR, PAIR), rows((2 * b + core) * BLOCK, BLOCK)]
        send_unit(0, p, q)
        for d, half in ((1, 0), (3, 1)):
            for ring in ("j", "i"):
                here = place(ring, RING - d, half)
                await_copy(here, "near", ring, d)
                send(here, here, target(ring, d), "first", *(("far", "j") if ring == "j" else ("late", "i")))
                if ring == "j":
                    send(here, here, sibling, "first", "shared")
        await_copy(total(2 * bytes_of(own[0])), "late", "j")
        for d, half in ((1, 1), (3, 0)):
            here = place("j", RING - d, half)
            send(here, here, sibling, "first", "shared")
        await_copy(total(2 * bytes_of(own[0])), "far", "j")
        for half in range(2):
            here = place("j", 2, half)
            send(here, here, sibling, "first", "shared")
        await_copy(total(4 * bytes_of(own[0])), "late", "i")
        await_copy(total(6 * bytes_of(own[0])), "shared")

    def send_unit(step, p, q):
        lag = turn(p - q, RING)
        at = slot("relay", step)

        @pl.when(lag != 0)
        def _():
            copy_at(unit.at[step], relay.at[step, lag - 1], GROUPS.index("relay") + step, at, device(step, p, p, z, core)).start()

    def pass_units_on(step, p, q):
        at, onward = slot("relay", step), slot("turned", step)

        @pl.when(p == q)
        def _():
            await_copy(relay.at[step], "relay", step)
            for d in (1, 2, 3):
                copy_at(relay.at[step, d - 1], turned.at[step], GROUPS.index("relay") + step, onward,
                        device(step, turn(p, RING - d), q, z, core)).start()
            turned[step] = unit[step]

    def await_turned(step, p, q):
        slot("turned", step)

        @pl.when(p != q)
        def _():
            await_copy(turned.at[step], "turned", step)

    def drain_units(step, p, q):
        def drain(ref):
            copy_at(ref, ref, GROUPS.index("relay") + step, 0, (grid_pos, y)).wait_send()

        pl.when(p != q)(lambda: drain(unit.at[step]))
        pl.when(p == q)(lambda: drain(relay.at[step]))

    def tile_j(p_at, chunk, core_at):
        return rows_j.at[1, rows(p_at * PAIR, PAIR), rows((2 * chunk + core_at) * BLOCK, BLOCK)]

    def tile_i(z_at, chunk, core_at):
        return rows_i.at[1, rows(z_at * BLOCK, BLOCK), rows((2 * chunk + core_at) * BLOCK, BLOCK)]

    def send_chunk(chunk, p, q):
        own = tile_j(p, chunk, core)
        for d in (1, 3):
            send(own, own, device(1, turn(p, d), q, z, core), "second", "near", chunk)
        send(own, own, device(1, p, q, z, other), "second", "shared again")
        for d in NEAR_FIRST:
            for to in (core, other):
                src = rows_j.at[1, rows(p * PAIR + to * BLOCK, BLOCK), rows((2 * chunk + core) * BLOCK, BLOCK)]
                send(src, tile_i(z, chunk, core), device(1, p, q, turn(z, d), to), "second", "slab again")
        tile_i(z, chunk, core)[...] = rows_j[1, rows(p * PAIR + core * BLOCK, BLOCK), rows((2 * chunk + core) * BLOCK, BLOCK)]

    def pass_chunk_on(chunk, p, q):
        await_copy(total(2 * bytes_of(tile_j(p, chunk, core))), "near", chunk)
        for d in (1, 3):
            here = tile_j(turn(p, RING - d), chunk, core)
            if (chunk % 2 == 0) == (d == 1):
                send(here, here, device(1, turn(p, d), q, z, core), "second", "far", chunk)
            send(here, here, device(1, p, q, z, other), "second", "shared again")

    def finish_chunk(chunk, p, q):
        here = tile_j(turn(p, 2), chunk, core)
        await_copy(here, "far", chunk)
        send(here, here, device(1, p, q, z, other), "second", "shared again")

    def await_chunks(p, q):
        await_copy(total(16 * bytes_of(tile_j(p, 0, other))), "shared again")
        for chunk in range(4):
            tile_i(z, chunk, other)[...] = rows_j[1, rows(p * PAIR + core * BLOCK, BLOCK), rows((2 * chunk + other) * BLOCK, BLOCK)]
        await_copy(total(24 * bytes_of(tile_i(z, 0, core))), "slab again")

    def square_terms(step, p, q):
        for half in range(2):
            lines = pl.ds(half * PAIR, PAIR)
            left = rows_i[step, lines, :]
            for d in FAR_FIRST:
                send_q[step, d - 1, lines, :] = nt_dot(left, rows_j[step, rows(turn(q, d) * PAIR, PAIR), :]).astype(jnp.bfloat16)
            for chunk in (2 * half, 2 * half + 1):
                part = pl.ds(chunk * BLOCK, BLOCK)
                for d in FAR_FIRST:
                    send(send_q.at[step, d - 1, part], got_q.at[step, d - 1, part], device(step, p, turn(q, d), z, core),
                         STEP_GROUPS[step], "q", step, chunk)
            own_q[lines, :] = nt_dot(left, rows_j[step, rows(q * PAIR, PAIR), :])

    def add_square(step, p, q, chunk):
        part = pl.ds(chunk * BLOCK, BLOCK)
        await_copy(got_q.at[step, :, part], "q", step, chunk)
        terms = own_q[part, :]
        for d in FAR_FIRST:
            terms += got_q[step, d - 1, part, :].astype(jnp.float32)
        for b in range(2):
            scale = keep(block_of(p, chunk, core), block_of(q, z, b)) * (1.0 / ORDER)
            square[step, part, rows(z * PAIR + b * BLOCK, BLOCK)] = (
                terms[:, b * BLOCK:(b + 1) * BLOCK] * scale).astype(jnp.bfloat16)
        block = square.at[step, part, rows(z * PAIR, PAIR)]
        for d in NEAR_FIRST:
            send(block, block, device(step, p, q, turn(z, d), core), STEP_GROUPS[step], "r", step, chunk)

    def cubic_terms(step, p, q, chunk):
        part = pl.ds(chunk * BLOCK, BLOCK)
        await_copy(got_q.at[step, :, part], "r", step, chunk)
        right = square[step, part, :]
        for d in FAR_FIRST:
            send_c[step, d - 1, chunk] = nt_dot(rows_j[step, rows(turn(q, d) * PAIR, PAIR), :], right).astype(jnp.bfloat16)
            send(send_c.at[step, d - 1, chunk], got_c.at[step, d - 1, chunk], device(step, p, turn(q, d), z, core),
                 STEP_GROUPS[step], "c", step, chunk)
        own_c[chunk] = nt_dot(rows_j[step, rows(q * PAIR, PAIR), :], right)

    def add_cubic(step, p, q, chunk):
        await_copy(got_c.at[step, :, chunk], "c", step, chunk)
        terms = own_c[chunk]
        for d in FAR_FIRST:
            terms += got_c[step, d - 1, chunk].astype(jnp.float32)
        cols = pl.ds(chunk * BLOCK, BLOCK)
        updated = 1.5 * turned[step, :, cols].astype(jnp.float32) - 0.5 * terms
        for b in range(2):
            part = updated[b * BLOCK:(b + 1) * BLOCK] * keep(block_of(q, z, b), block_of(p, chunk, core))
            if step == 0:
                unit[1, pl.ds(b * BLOCK, BLOCK), cols] = part.astype(jnp.bfloat16)
            else:
                final[chunk, pl.ds(b * BLOCK, BLOCK), :] = part
        if step == 0:
            tile_j(q, chunk, core)[...] = unit[1, :, cols]
            send_chunk(chunk, q, p)
        else:
            place = out.at[:, rows((2 * chunk + core) * BLOCK, BLOCK)]
            send(final.at[chunk, rows(other * BLOCK, BLOCK)], place, device(step, p, q, z, other), STEP_GROUPS[step], "f")
            store = pltpu.make_async_copy(final.at[chunk, rows(core * BLOCK, BLOCK)], place, store_sem.at[chunk])
            store.start()
            stores.append(store)

    for step in range(STEPS):
        p, q = (x, y) if step == 0 else (y, x)
        at = (step, p, q)
        if step == 0:
            gather_first(p, q)
        else:
            send_unit(*at)
            finish_chunk(0, p, q)
            pass_chunk_on(2, p, q)
            finish_chunk(1, p, q)
            pass_chunk_on(3, p, q)
            finish_chunk(2, p, q)
            finish_chunk(3, p, q)
            await_chunks(p, q)
        square_terms(*at)
        pass_units_on(*at)
        add_square(*at, 0)
        add_square(*at, 1)
        add_square(*at, 2)
        cubic_terms(*at, 0)
        add_square(*at, 3)
        cubic_terms(*at, 1)
        cubic_terms(*at, 2)
        await_turned(*at)
        add_cubic(*at, 0)
        cubic_terms(*at, 3)
        add_cubic(*at, 1)
        if step == 0:
            pass_chunk_on(0, q, p)
        add_cubic(*at, 2)
        if step == 0:
            pass_chunk_on(1, q, p)
        add_cubic(*at, 3)

    await_copy(final.at[:, pl.ds(0, BLOCK)], "f")
    for group, size in groups.items():
        copy_at(total(size), total(size), GROUPS.index(group), 0, (grid_pos, y)).wait_send()
    for store in stores:
        store.wait()
    assert len(slots) == ARRIVALS, len(slots)
    for step in range(STEPS):
        p, q = (x, y) if step == 0 else (y, x)
        drain_units(step, p, q)


def per_device(density, pattern):
    bf16, f32 = jnp.bfloat16, jnp.float32
    quarter = ORDER // RING
    return pl.pallas_call(
        kernel,
        out_shape=jax.ShapeDtypeStruct(density.shape, f32),
        in_specs=[pl.BlockSpec(memory_space=pl.ANY)] * 2,
        out_specs=pl.BlockSpec(memory_space=pl.ANY),
        scratch_shapes=[
            pltpu.VMEM(density.shape, bf16),
            pltpu.SMEM(pattern.shape, jnp.int32),
            pltpu.VMEM((STEPS, 4 * BLOCK, quarter), bf16),
            pltpu.VMEM((STEPS, 8 * BLOCK, quarter), bf16),
            pltpu.VMEM((STEPS, 3, 4 * BLOCK, PAIR), bf16),
            pltpu.VMEM((STEPS, 3, 4 * BLOCK, PAIR), bf16),
            pltpu.VMEM((4 * BLOCK, PAIR), f32),
            pltpu.VMEM((STEPS, 4 * BLOCK, quarter), bf16),
            pltpu.VMEM((STEPS, 3, 4, PAIR, BLOCK), bf16),
            pltpu.VMEM((STEPS, 3, 4, PAIR, BLOCK), bf16),
            pltpu.VMEM((4, PAIR, BLOCK), f32),
            pltpu.VMEM((STEPS, PAIR, 4 * BLOCK), bf16),
            pltpu.VMEM((STEPS, 3, PAIR, 4 * BLOCK), bf16),
            pltpu.VMEM((STEPS, PAIR, 4 * BLOCK), bf16),
            pltpu.VMEM((4, PAIR, BLOCK), f32),
            pltpu.SemaphoreType.DMA((2,)),
            pltpu.SemaphoreType.DMA((4,)),
            pltpu.SemaphoreType.DMA((len(GROUPS),)),
            pltpu.SemaphoreType.DMA((ARRIVALS,)),
        ],
        compiler_params=pltpu.CompilerParams(
            collective_id=0, has_side_effects=True, vmem_limit_bytes=56 * 2**20
        ),
        name="polar_steps",
    )(density, pattern)


def solution(mesh):
    placed = (P("grid", "rep"), P())
    return jax.shard_map(
        per_device, mesh=mesh, in_specs=placed, out_specs=P("grid", "rep"), check_vma=False
    )
```

time: 389 us -> 89.8 us (0.23)
  waiting for transfers between devices: 334 us -> 0 us
  Pallas kernels: 0 us -> 87.1 us
  matrix products: 30.6 us -> 0 us
  between operations: 13.5 us -> 0.01 us
  other arithmetic: 9.76 us -> 0 us
    all_gather x4 -> x0, waiting for transfers between devices: 218 us -> none  [product(): lax.all_gather(right_tile, 'grid', axis=0, tiled=True)]
    reduce_scatter x4 -> x0, waiting for transfers between devices: 116 us -> none  [product(): lax.psum_scatter(partial_terms, 'rep', scatter_dimension=1, tiled=True)]
    pallas_call x0 -> x1, Pallas kernels: none -> 87.1 us  [per_device(): pl.pallas_call(kernel, out_shape=jax.ShapeDtypeStruct(density.shape, f32)...]
    dot_general x4 -> x0, matrix products: 30.6 us -> none  [make_columns(): lax.dot_general(left_tile, part_rows, (((1,), (1,)), ((), ())), preferred...]
    convert_element_type x3 -> x0, other arithmetic: 5.46 us -> none  [the longest x2 3.6 us: per_device(): jnp.where(tile_keep, product(state, state) / order, jnp.float32(0.0))]
  transfers between devices with their start and end apart: 8 -> 0, of which waited for: 8 -> 0; matrix products, arithmetic and copies ran while one was open for 0% -> 0% of each run, Pallas kernels for 0% -> 0%
where the time goes in v2:
time: 89.8 us; the launch traced here: 89 us
  Pallas kernels  87.1 us (97%)
  local copies, waits for them, and re-layouts  1.89 us (2%)
    pallas_call x1, Pallas kernels, per_device(): pl.pallas_call(kernel, out_shape=jax.ShapeDtypeStruct(density.shape, f32)...  87.1 us
    unnamed x1, local copies, waits for them, and re-layouts  1.89 us

profile of v2, /device:TPU:1, one launch (start us, length us, event | category | flops | bytes accessed | tf_op | source)
XLA Modules:
  0.0 89.0 jit_solution(15521129183699068633)
XLA Ops:
  0.0 87.1 %polar_steps.1 = f32[128,1024]{1,0:T(8,128)} custom-call(bf16[128,1024]{1,0:T(8,128)(2,1)} %density.1, s32[32,32]{1,0:T(8,128)} %pattern_in.1), custom_call_target="tpu_custom_call" | custom-call | tf_op jit(solution)/shard_map/polar_steps/pallas_call | solution.py:322
  87.1 1.9 %copy.4 = f32[128,1024]{1,0:T(8,128)} copy(f32[128,1024]{1,0:T(8,128)} %polar_steps.1) | data formatting | bytes 1048576

commit v3 on v2

--- a/solution.py
+++ b/solution.py
@@ -19,7 +19,9 @@
 
 GROUPS = ("first", "second", "step 1", "step 2", "relay", "relay again")
 STEP_GROUPS = GROUPS[2:4]
-ARRIVALS = 48
+MERGED = ((0, 0), (0, 1), (0, 2), (0, 3))
+ARRIVALS = 56 + len(MERGED)
+DIRECT = (2, 3)
 
 
 def nt_dot(left, right):
@@ -30,8 +32,8 @@
     return outer * 8 + z * 2 + core
 
 
-def kernel(density, pattern_in, out, loaded, pattern, rows_i, rows_j, send_q, got_q, own_q, square, send_c, got_c, own_c,
-           unit, relay, turned, final, load_sem, store_sem, send_sem, recv_sem):
+def kernel(density, pattern_in, out, loaded, pattern, rows_i, rows_j, send_q, got_q, terms_q, square, send_c, got_c, terms_c, passing,
+           unit, relay, turned, final, load_sem, send_sem, recv_sem):
     grid_pos = lax.axis_index("grid")
     y = lax.axis_index("rep")
     x = grid_pos // 8
@@ -83,8 +85,6 @@
         masked = loaded[:, cols].astype(jnp.float32) * keep(block_of(x, z, core), y * 8 + b)
         rows_j[0, mine, cols] = masked.astype(jnp.bfloat16)
     pl.semaphore_wait(barrier, len(partners))
-
-    stores = []
 
     def total(size):
         return rows_j.at[:, pl.ds(0, size // (2 * STEPS * rows_j.shape[2]))]
@@ -123,7 +123,7 @@
         await_copy(rows_j.at[0, rows(p * PAIR + other * BLOCK, BLOCK)], "pair")
         for b in range(4):
             unit[0, :, pl.ds(b * BLOCK, BLOCK)] = rows_j[0, rows(p * PAIR, PAIR), rows((2 * b + core) * BLOCK, BLOCK)]
-        send_unit(0, p, q)
+        send_unit(0, p, q, pl.ds(0, 4 * BLOCK))
         for d, half in ((1, 0), (3, 1)):
             for ring in ("j", "i"):
                 here = place(ring, RING - d, half)
@@ -142,13 +142,14 @@
         await_copy(total(4 * bytes_of(own[0])), "late", "i")
         await_copy(total(6 * bytes_of(own[0])), "shared")
 
-    def send_unit(step, p, q):
+    def send_unit(step, p, q, cols):
         lag = turn(p - q, RING)
         at = slot("relay", step)
 
         @pl.when(lag != 0)
         def _():
-            copy_at(unit.at[step], relay.at[step, lag - 1], GROUPS.index("relay") + step, at, device(step, p, p, z, core)).start()
+            copy_at(unit.at[step, :, cols], relay.at[step, lag - 1, :, cols], GROUPS.index("relay") + step, at,
+                    device(step, p, p, z, core)).start()
 
     def pass_units_on(step, p, q):
         at, onward = slot("relay", step), slot("turned", step)
@@ -185,6 +186,8 @@
         own = tile_j(p, chunk, core)
         for d in (1, 3):
             send(own, own, device(1, turn(p, d), q, z, core), "second", "near", chunk)
+        if chunk in DIRECT:
+            send(own, own, device(1, turn(p, 2), q, z, core), "second", "far", chunk)
         send(own, own, device(1, p, q, z, other), "second", "shared again")
         for d in NEAR_FIRST:
             for to in (core, other):
@@ -196,7 +199,7 @@
         await_copy(total(2 * bytes_of(tile_j(p, chunk, core))), "near", chunk)
         for d in (1, 3):
             here = tile_j(turn(p, RING - d), chunk, core)
-            if (chunk % 2 == 0) == (d == 1):
+            if chunk not in DIRECT and (chunk % 2 == 0) == (d == 1):
                 send(here, here, device(1, turn(p, d), q, z, core), "second", "far", chunk)
             send(here, here, device(1, p, q, z, other), "second", "shared again")
 
@@ -214,44 +217,65 @@
     def square_terms(step, p, q):
         for half in range(2):
             lines = pl.ds(half * PAIR, PAIR)
-            left = rows_i[step, lines, :]
-            for d in FAR_FIRST:
-                send_q[step, d - 1, lines, :] = nt_dot(left, rows_j[step, rows(turn(q, d) * PAIR, PAIR), :]).astype(jnp.bfloat16)
-            for chunk in (2 * half, 2 * half + 1):
-                part = pl.ds(chunk * BLOCK, BLOCK)
+            terms_q[lines, :] = nt_dot(rows_i[step, lines, :], rows_j[step])
+            send_q[step, lines, :] = terms_q[lines, :].astype(jnp.bfloat16)
+            for strip in range(4 * half, 4 * half + 4):
+                part = pl.ds(strip * HALF, HALF)
                 for d in FAR_FIRST:
-                    send(send_q.at[step, d - 1, part], got_q.at[step, d - 1, part], device(step, p, turn(q, d), z, core),
-                         STEP_GROUPS[step], "q", step, chunk)
-            own_q[lines, :] = nt_dot(left, rows_j[step, rows(q * PAIR, PAIR), :])
-
-    def add_square(step, p, q, chunk):
-        part = pl.ds(chunk * BLOCK, BLOCK)
-        await_copy(got_q.at[step, :, part], "q", step, chunk)
-        terms = own_q[part, :]
+                    send(send_q.at[step, part, rows(turn(q, d) * PAIR, PAIR)], got_q.at[step, d - 1, part],
+                         device(step, p, turn(q, d), z, core), STEP_GROUPS[step], "q", step, strip)
+
+    def add_square(step, p, q, strip):
+        part = pl.ds(strip * HALF, HALF)
+        await_copy(got_q.at[step, :, part], "q", step, strip)
+        terms = terms_q[part, rows(q * PAIR, PAIR)]
         for d in FAR_FIRST:
             terms += got_q[step, d - 1, part, :].astype(jnp.float32)
         for b in range(2):
-            scale = keep(block_of(p, chunk, core), block_of(q, z, b)) * (1.0 / ORDER)
+            scale = keep(block_of(p, strip // 2, core), block_of(q, z, b)) * (1.0 / ORDER)
             square[step, part, rows(z * PAIR + b * BLOCK, BLOCK)] = (
                 terms[:, b * BLOCK:(b + 1) * BLOCK] * scale).astype(jnp.bfloat16)
         block = square.at[step, part, rows(z * PAIR, PAIR)]
         for d in NEAR_FIRST:
-            send(block, block, device(step, p, q, turn(z, d), core), STEP_GROUPS[step], "r", step, chunk)
+            send(block, block, device(step, p, q, turn(z, d), core), STEP_GROUPS[step], "r", step, strip // 2)
 
     def cubic_terms(step, p, q, chunk):
         part = pl.ds(chunk * BLOCK, BLOCK)
         await_copy(got_q.at[step, :, part], "r", step, chunk)
-        right = square[step, part, :]
-        for d in FAR_FIRST:
-            send_c[step, d - 1, chunk] = nt_dot(rows_j[step, rows(turn(q, d) * PAIR, PAIR), :], right).astype(jnp.bfloat16)
-            send(send_c.at[step, d - 1, chunk], got_c.at[step, d - 1, chunk], device(step, p, turn(q, d), z, core),
-                 STEP_GROUPS[step], "c", step, chunk)
-        own_c[chunk] = nt_dot(rows_j[step, rows(q * PAIR, PAIR), :], right)
+        for b in range(2):
+            lines = pl.ds(b * 512, 512)
+            terms_c[chunk, lines] = nt_dot(rows_j[step, lines, :], square[step, part, :])
+            send_c[step, chunk, lines] = terms_c[chunk, lines].astype(jnp.bfloat16)
+        if (step, chunk) in MERGED:
+            for b, d in enumerate((1, 3)):
+                send(send_c.at[step, chunk, rows(turn(q, 2) * PAIR + b * BLOCK, BLOCK)], passing.at[chunk, b],
+                     device(step, p, turn(q, d), z, core), STEP_GROUPS[step], "via", step, chunk)
+            for b, d in enumerate((1, 3)):
+                send_cubic(step, p, q, chunk, 1 - b, d)
+        else:
+            for d in FAR_FIRST:
+                send(send_c.at[step, chunk, rows(turn(q, d) * PAIR, PAIR)], got_c.at[step, d - 1, chunk],
+                     device(step, p, turn(q, d), z, core), STEP_GROUPS[step], "c", step, chunk)
+
+    def send_cubic(step, p, q, chunk, b, d):
+        send(send_c.at[step, chunk, rows(turn(q, d) * PAIR + b * BLOCK, BLOCK)],
+             got_c.at[step, d - 1, chunk, pl.ds(b * BLOCK, BLOCK)],
+             device(step, p, turn(q, d), z, core), STEP_GROUPS[step], "c", step, chunk)
+
+    def merge_terms(step, p, q, chunk):
+        if (step, chunk) not in MERGED:
+            return
+        await_copy(passing.at[chunk], "via", step, chunk)
+        for b, d in enumerate((1, 3)):
+            half = rows(turn(q, d) * PAIR + b * BLOCK, BLOCK)
+            send_c[step, chunk, half, :] = (terms_c[chunk, half, :] + passing[chunk, b].astype(jnp.float32)).astype(jnp.bfloat16)
+            send_cubic(step, p, q, chunk, b, d)
 
     def add_cubic(step, p, q, chunk):
-        await_copy(got_c.at[step, :, chunk], "c", step, chunk)
-        terms = own_c[chunk]
-        for d in FAR_FIRST:
+        sources = (1, 3) if (step, chunk) in MERGED else FAR_FIRST
+        await_copy(got_c.at[step, pl.ds(0, len(sources)), chunk], "c", step, chunk)
+        terms = terms_c[chunk, rows(q * PAIR, PAIR), :]
+        for d in sources:
             terms += got_c[step, d - 1, chunk].astype(jnp.float32)
         cols = pl.ds(chunk * BLOCK, BLOCK)
         updated = 1.5 * turned[step, :, cols].astype(jnp.float32) - 0.5 * terms
@@ -264,12 +288,11 @@
         if step == 0:
             tile_j(q, chunk, core)[...] = unit[1, :, cols]
             send_chunk(chunk, q, p)
+            send_unit(1, q, p, cols)
         else:
             place = out.at[:, rows((2 * chunk + core) * BLOCK, BLOCK)]
             send(final.at[chunk, rows(other * BLOCK, BLOCK)], place, device(step, p, q, z, other), STEP_GROUPS[step], "f")
-            store = pltpu.make_async_copy(final.at[chunk, rows(core * BLOCK, BLOCK)], place, store_sem.at[chunk])
-            store.start()
-            stores.append(store)
+            place[...] = final[chunk, rows(core * BLOCK, BLOCK), :]
 
     for step in range(STEPS):
         p, q = (x, y) if step == 0 else (y, x)
@@ -277,27 +300,33 @@
         if step == 0:
             gather_first(p, q)
         else:
-            send_unit(*at)
             finish_chunk(0, p, q)
             pass_chunk_on(2, p, q)
             finish_chunk(1, p, q)
             pass_chunk_on(3, p, q)
             finish_chunk(2, p, q)
             finish_chunk(3, p, q)
+            pass_units_on(*at)
             await_chunks(p, q)
         square_terms(*at)
-        pass_units_on(*at)
-        add_square(*at, 0)
-        add_square(*at, 1)
-        add_square(*at, 2)
+        for strip in range(5):
+            add_square(*at, strip)
+            if strip == 0 and step == 0:
+                pass_units_on(*at)
         cubic_terms(*at, 0)
-        add_square(*at, 3)
+        add_square(*at, 5)
+        add_square(*at, 6)
         cubic_terms(*at, 1)
+        merge_terms(*at, 0)
+        add_square(*at, 7)
         cubic_terms(*at, 2)
+        merge_terms(*at, 1)
         await_turned(*at)
         add_cubic(*at, 0)
         cubic_terms(*at, 3)
+        merge_terms(*at, 2)
         add_cubic(*at, 1)
+        merge_terms(*at, 3)
         if step == 0:
             pass_chunk_on(0, q, p)
         add_cubic(*at, 2)
@@ -308,8 +337,6 @@
     await_copy(final.at[:, pl.ds(0, BLOCK)], "f")
     for group, size in groups.items():
         copy_at(total(size), total(size), GROUPS.index(group), 0, (grid_pos, y)).wait_send()
-    for store in stores:
-        store.wait()
     assert len(slots) == ARRIVALS, len(slots)
     for step in range(STEPS):
         p, q = (x, y) if step == 0 else (y, x)
@@ -321,27 +348,27 @@
     quarter = ORDER // RING
     return pl.pallas_call(
         kernel,
-        out_shape=jax.ShapeDtypeStruct(density.shape, f32),
+        out_shape=pltpu.VMEM(density.shape, f32),
         in_specs=[pl.BlockSpec(memory_space=pl.ANY)] * 2,
-        out_specs=pl.BlockSpec(memory_space=pl.ANY),
+        out_specs=pl.BlockSpec(memory_space=pltpu.VMEM),
         scratch_shapes=[
             pltpu.VMEM(density.shape, bf16),
             pltpu.SMEM(pattern.shape, jnp.int32),
             pltpu.VMEM((STEPS, 4 * BLOCK, quarter), bf16),
             pltpu.VMEM((STEPS, 8 * BLOCK, quarter), bf16),
+            pltpu.VMEM((STEPS, 4 * BLOCK, quarter), bf16),
             pltpu.VMEM((STEPS, 3, 4 * BLOCK, PAIR), bf16),
-            pltpu.VMEM((STEPS, 3, 4 * BLOCK, PAIR), bf16),
-            pltpu.VMEM((4 * BLOCK, PAIR), f32),
+            pltpu.VMEM((4 * BLOCK, quarter), f32),
             pltpu.VMEM((STEPS, 4 * BLOCK, quarter), bf16),
+            pltpu.VMEM((STEPS, 4, quarter, BLOCK), bf16),
             pltpu.VMEM((STEPS, 3, 4, PAIR, BLOCK), bf16),
-            pltpu.VMEM((STEPS, 3, 4, PAIR, BLOCK), bf16),
-            pltpu.VMEM((4, PAIR, BLOCK), f32),
+            pltpu.VMEM((4, quarter, BLOCK), f32),
+            pltpu.VMEM((4, 2, BLOCK, BLOCK), bf16),
             pltpu.VMEM((STEPS, PAIR, 4 * BLOCK), bf16),
             pltpu.VMEM((STEPS, 3, PAIR, 4 * BLOCK), bf16),
             pltpu.VMEM((STEPS, PAIR, 4 * BLOCK), bf16),
             pltpu.VMEM((4, PAIR, BLOCK), f32),
             pltpu.SemaphoreType.DMA((2,)),
-            pltpu.SemaphoreType.DMA((4,)),
             pltpu.SemaphoreType.DMA((len(GROUPS),)),
             pltpu.SemaphoreType.DMA((ARRIVALS,)),
         ],

time: 89.8 us -> 82.9 us (0.923)
  Pallas kernels: 87.1 us -> 81.9 us
  local copies, waits for them, and re-layouts: 1.89 us -> 0.8 us
    pallas_call x1, Pallas kernels: 87.1 us -> 81.9 us  [per_device(): pl.pallas_call(kernel, out_shape=pltpu.VMEM(density.shape, f32), in_specs...]
    unnamed x1, local copies, waits for them, and re-layouts: 1.89 us -> 0.8 us
where the time goes in v3:
time: 82.9 us; the launch traced here: 82.7 us
  Pallas kernels  81.9 us (99%)
    pallas_call x1, Pallas kernels, per_device(): pl.pallas_call(kernel, out_shape=pltpu.VMEM(density.shape, f32), in_specs...  81.9 us

profile of v3, /device:TPU:1, one launch (start us, length us, event | category | flops | bytes accessed | tf_op | source)
XLA Modules:
  0.0 82.7 jit_solution(8214029051166680467)
XLA Ops:
  0.0 81.9 %polar_steps.1 = f32[128,1024]{1,0:T(8,128)S(1)} custom-call(bf16[128,1024]{1,0:T(8,128)(2,1)} %density.1, s32[32,32]{1,0:T(8,128)} %pattern_in.1), custom_call_target="tpu_custom_call" | custom-call | tf_op jit(solution)/shard_map/polar_steps/pallas_call | solution.py:349
  81.9 0.8 copy.4

commit v4 on v3

--- a/solution.py
+++ b/solution.py
@@ -20,7 +20,7 @@
 GROUPS = ("first", "second", "step 1", "step 2", "relay", "relay again")
 STEP_GROUPS = GROUPS[2:4]
 MERGED = ((0, 0), (0, 1), (0, 2), (0, 3))
-ARRIVALS = 56 + len(MERGED)
+ARRIVALS = 66 + len(MERGED)
 DIRECT = (2, 3)
 
 
@@ -32,8 +32,8 @@
     return outer * 8 + z * 2 + core
 
 
-def kernel(density, pattern_in, out, loaded, pattern, rows_i, rows_j, send_q, got_q, terms_q, square, send_c, got_c, terms_c, passing,
-           unit, relay, turned, final, load_sem, send_sem, recv_sem):
+def kernel(density, pattern_in, out, loaded, pattern, rows_i, rows_j, send_q, got_q, terms_q, square, send_c, got_c, terms_c, passing, got_f, got_own, turned_rest,
+           unit, relay, turned, load_sem, send_sem, recv_sem):
     grid_pos = lax.axis_index("grid")
     y = lax.axis_index("rep")
     x = grid_pos // 8
@@ -66,7 +66,7 @@
     barrier = pltpu.get_barrier_semaphore()
     partners = [device(0, x, y, z, other)]
     for d in (1, 2, 3):
-        partners += [device(0, turn(x, d), y, z, core), device(0, x, turn(y, d), z, core),
+        partners += [device(0, turn(x, d), y, z, core), device(0, turn(x, d), y, z, other), device(0, x, turn(y, d), z, core),
                      device(0, x, y, turn(z, d), core), device(0, x, y, turn(z, d), other)]
     for partner in partners:
         pl.semaphore_signal(barrier, inc=1, device_id=partner, device_id_type=MESH)
@@ -184,15 +184,15 @@
 
     def send_chunk(chunk, p, q):
         own = tile_j(p, chunk, core)
+        if chunk in DIRECT:
+            send(own, own, device(1, turn(p, 2), q, z, core), "second", "far", chunk)
         for d in (1, 3):
             send(own, own, device(1, turn(p, d), q, z, core), "second", "near", chunk)
-        if chunk in DIRECT:
-            send(own, own, device(1, turn(p, 2), q, z, core), "second", "far", chunk)
-        send(own, own, device(1, p, q, z, other), "second", "shared again")
+        send(own, own, device(1, p, q, z, other), "second", "shared again", chunk)
         for d in NEAR_FIRST:
             for to in (core, other):
                 src = rows_j.at[1, rows(p * PAIR + to * BLOCK, BLOCK), rows((2 * chunk + core) * BLOCK, BLOCK)]
-                send(src, tile_i(z, chunk, core), device(1, p, q, turn(z, d), to), "second", "slab again")
+                send(src, tile_i(z, chunk, core), device(1, p, q, turn(z, d), to), "second", "slab again", chunk)
         tile_i(z, chunk, core)[...] = rows_j[1, rows(p * PAIR + core * BLOCK, BLOCK), rows((2 * chunk + core) * BLOCK, BLOCK)]
 
     def pass_chunk_on(chunk, p, q):
@@ -201,18 +201,17 @@
             here = tile_j(turn(p, RING - d), chunk, core)
             if chunk not in DIRECT and (chunk % 2 == 0) == (d == 1):
                 send(here, here, device(1, turn(p, d), q, z, core), "second", "far", chunk)
-            send(here, here, device(1, p, q, z, other), "second", "shared again")
+            send(here, here, device(1, p, q, z, other), "second", "shared again", chunk)
 
     def finish_chunk(chunk, p, q):
         here = tile_j(turn(p, 2), chunk, core)
         await_copy(here, "far", chunk)
-        send(here, here, device(1, p, q, z, other), "second", "shared again")
-
-    def await_chunks(p, q):
-        await_copy(total(16 * bytes_of(tile_j(p, 0, other))), "shared again")
-        for chunk in range(4):
-            tile_i(z, chunk, other)[...] = rows_j[1, rows(p * PAIR + core * BLOCK, BLOCK), rows((2 * chunk + other) * BLOCK, BLOCK)]
-        await_copy(total(24 * bytes_of(tile_i(z, 0, core))), "slab again")
+        send(here, here, device(1, p, q, z, other), "second", "shared again", chunk)
+
+    def await_chunk(chunk, p, q):
+        await_copy(total(4 * bytes_of(tile_j(p, 0, other))), "shared again", chunk)
+        tile_i(z, chunk, other)[...] = rows_j[1, rows(p * PAIR + core * BLOCK, BLOCK), rows((2 * chunk + other) * BLOCK, BLOCK)]
+        await_copy(total(6 * bytes_of(tile_i(z, 0, core))), "slab again", chunk)
 
     def square_terms(step, p, q):
         for half in range(2):
@@ -242,8 +241,8 @@
     def cubic_terms(step, p, q, chunk):
         part = pl.ds(chunk * BLOCK, BLOCK)
         await_copy(got_q.at[step, :, part], "r", step, chunk)
-        for b in range(2):
-            lines = pl.ds(b * 512, 512)
+        for b in range(4):
+            lines = pl.ds(b * PAIR, PAIR)
             terms_c[chunk, lines] = nt_dot(rows_j[step, lines, :], square[step, part, :])
             send_c[step, chunk, lines] = terms_c[chunk, lines].astype(jnp.bfloat16)
         if (step, chunk) in MERGED:
@@ -252,14 +251,21 @@
                      device(step, p, turn(q, d), z, core), STEP_GROUPS[step], "via", step, chunk)
             for b, d in enumerate((1, 3)):
                 send_cubic(step, p, q, chunk, 1 - b, d)
+        elif step == 0:
+            for d in FAR_FIRST:
+                send(send_c.at[0, chunk, rows(turn(q, d) * PAIR, PAIR)], got_c.at[d - 1, chunk],
+                     device(0, p, turn(q, d), z, core), STEP_GROUPS[0], "c", 0, chunk)
         else:
             for d in FAR_FIRST:
-                send(send_c.at[step, chunk, rows(turn(q, d) * PAIR, PAIR)], got_c.at[step, d - 1, chunk],
-                     device(step, p, turn(q, d), z, core), STEP_GROUPS[step], "c", step, chunk)
+                for to in (core, other):
+                    send(send_c.at[1, chunk, rows(turn(q, d) * PAIR + to * BLOCK, BLOCK)], got_f.at[d - 1, chunk, core],
+                         device(1, p, turn(q, d), z, to), STEP_GROUPS[1], "c", 1, chunk)
+            send(terms_c.at[chunk, rows(q * PAIR + other * BLOCK, BLOCK)], got_own.at[chunk], device(1, p, q, z, other),
+                 STEP_GROUPS[1], "own", chunk)
 
     def send_cubic(step, p, q, chunk, b, d):
         send(send_c.at[step, chunk, rows(turn(q, d) * PAIR + b * BLOCK, BLOCK)],
-             got_c.at[step, d - 1, chunk, pl.ds(b * BLOCK, BLOCK)],
+             got_c.at[d - 1, chunk, pl.ds(b * BLOCK, BLOCK)],
              device(step, p, turn(q, d), z, core), STEP_GROUPS[step], "c", step, chunk)
 
     def merge_terms(step, p, q, chunk):
@@ -271,28 +277,37 @@
             send_c[step, chunk, half, :] = (terms_c[chunk, half, :] + passing[chunk, b].astype(jnp.float32)).astype(jnp.bfloat16)
             send_cubic(step, p, q, chunk, b, d)
 
-    def add_cubic(step, p, q, chunk):
-        sources = (1, 3) if (step, chunk) in MERGED else FAR_FIRST
-        await_copy(got_c.at[step, pl.ds(0, len(sources)), chunk], "c", step, chunk)
+    def add_cubic(p, q, chunk):
+        sources = (1, 3) if (0, chunk) in MERGED else FAR_FIRST
+        await_copy(got_c.at[pl.ds(0, len(sources)), chunk], "c", 0, chunk)
         terms = terms_c[chunk, rows(q * PAIR, PAIR), :]
         for d in sources:
-            terms += got_c[step, d - 1, chunk].astype(jnp.float32)
+            terms += got_c[d - 1, chunk].astype(jnp.float32)
         cols = pl.ds(chunk * BLOCK, BLOCK)
-        updated = 1.5 * turned[step, :, cols].astype(jnp.float32) - 0.5 * terms
+        updated = 1.5 * turned[0, :, cols].astype(jnp.float32) - 0.5 * terms
         for b in range(2):
             part = updated[b * BLOCK:(b + 1) * BLOCK] * keep(block_of(q, z, b), block_of(p, chunk, core))
-            if step == 0:
-                unit[1, pl.ds(b * BLOCK, BLOCK), cols] = part.astype(jnp.bfloat16)
-            else:
-                final[chunk, pl.ds(b * BLOCK, BLOCK), :] = part
-        if step == 0:
-            tile_j(q, chunk, core)[...] = unit[1, :, cols]
-            send_chunk(chunk, q, p)
-            send_unit(1, q, p, cols)
-        else:
-            place = out.at[:, rows((2 * chunk + core) * BLOCK, BLOCK)]
-            send(final.at[chunk, rows(other * BLOCK, BLOCK)], place, device(step, p, q, z, other), STEP_GROUPS[step], "f")
-            place[...] = final[chunk, rows(core * BLOCK, BLOCK), :]
+            unit[1, pl.ds(b * BLOCK, BLOCK), cols] = part.astype(jnp.bfloat16)
+        tile_j(q, chunk, core)[...] = unit[1, :, cols]
+        send_chunk(chunk, q, p)
+        send_unit(1, q, p, cols)
+
+    def share_turned(p, q):
+        send(turned.at[1, rows(other * BLOCK, BLOCK)], turned_rest, device(1, p, q, z, other), STEP_GROUPS[1], "turned rest")
+
+    def put_out(p, q, chunk):
+        if chunk == 0:
+            await_copy(turned_rest, "turned rest")
+        await_copy(total(6 * bytes_of(got_own.at[0]) // 2), "c", 1, chunk)
+        await_copy(got_own.at[chunk], "own", chunk)
+        cols = pl.ds(chunk * BLOCK, BLOCK)
+        mine = rows(core * BLOCK, BLOCK)
+        for by, terms, state in ((core, terms_c[chunk, rows(q * PAIR + core * BLOCK, BLOCK), :], turned[1, mine, cols]),
+                                 (other, got_own[chunk], turned_rest[:, cols])):
+            for d in FAR_FIRST:
+                terms += got_f[d - 1, chunk, by].astype(jnp.float32)
+            updated = 1.5 * state.astype(jnp.float32) - 0.5 * terms
+            out[:, rows((2 * chunk + by) * BLOCK, BLOCK)] = updated * keep(block_of(q, z, core), block_of(p, chunk, by))
 
     for step in range(STEPS):
         p, q = (x, y) if step == 0 else (y, x)
@@ -306,8 +321,9 @@
             pass_chunk_on(3, p, q)
             finish_chunk(2, p, q)
             finish_chunk(3, p, q)
+            for chunk in range(4):
+                await_chunk(chunk, p, q)
             pass_units_on(*at)
-            await_chunks(p, q)
         square_terms(*at)
         for strip in range(5):
             add_square(*at, strip)
@@ -317,24 +333,31 @@
         add_square(*at, 5)
         add_square(*at, 6)
         cubic_terms(*at, 1)
-        merge_terms(*at, 0)
-        add_square(*at, 7)
-        cubic_terms(*at, 2)
-        merge_terms(*at, 1)
-        await_turned(*at)
-        add_cubic(*at, 0)
-        cubic_terms(*at, 3)
-        merge_terms(*at, 2)
-        add_cubic(*at, 1)
-        merge_terms(*at, 3)
         if step == 0:
+            merge_terms(*at, 0)
+            add_square(*at, 7)
+            cubic_terms(*at, 2)
+            merge_terms(*at, 1)
+            await_turned(*at)
+            add_cubic(p, q, 0)
+            cubic_terms(*at, 3)
+            merge_terms(*at, 2)
+            add_cubic(p, q, 1)
+            merge_terms(*at, 3)
             pass_chunk_on(0, q, p)
-        add_cubic(*at, 2)
-        if step == 0:
+            add_cubic(p, q, 2)
             pass_chunk_on(1, q, p)
-        add_cubic(*at, 3)
-
-    await_copy(final.at[:, pl.ds(0, BLOCK)], "f")
+            add_cubic(p, q, 3)
+        else:
+            add_square(*at, 7)
+            await_turned(*at)
+            share_turned(p, q)
+            cubic_terms(*at, 2)
+            put_out(p, q, 0)
+            cubic_terms(*at, 3)
+            for chunk in (1, 2, 3):
+                put_out(p, q, chunk)
+
     for group, size in groups.items():
         copy_at(total(size), total(size), GROUPS.index(group), 0, (grid_pos, y)).wait_send()
     assert len(slots) == ARRIVALS, len(slots)
@@ -361,13 +384,15 @@
             pltpu.VMEM((4 * BLOCK, quarter), f32),
             pltpu.VMEM((STEPS, 4 * BLOCK, quarter), bf16),
             pltpu.VMEM((STEPS, 4, quarter, BLOCK), bf16),
-            pltpu.VMEM((STEPS, 3, 4, PAIR, BLOCK), bf16),
+            pltpu.VMEM((3, 4, PAIR, BLOCK), bf16),
             pltpu.VMEM((4, quarter, BLOCK), f32),
             pltpu.VMEM((4, 2, BLOCK, BLOCK), bf16),
+            pltpu.VMEM((3, 4, 2, BLOCK, BLOCK), bf16),
+            pltpu.VMEM((4, BLOCK, BLOCK), f32),
+            pltpu.VMEM((BLOCK, 4 * BLOCK), bf16),
             pltpu.VMEM((STEPS, PAIR, 4 * BLOCK), bf16),
             pltpu.VMEM((STEPS, 3, PAIR, 4 * BLOCK), bf16),
             pltpu.VMEM((STEPS, PAIR, 4 * BLOCK), bf16),
-            pltpu.VMEM((4, PAIR, BLOCK), f32),
             pltpu.SemaphoreType.DMA((2,)),
             pltpu.SemaphoreType.DMA((len(GROUPS),)),
             pltpu.SemaphoreType.DMA((ARRIVALS,)),

time: 82.9 us -> 81.7 us (0.986)
  Pallas kernels: 81.9 us -> 80.8 us
    pallas_call x1, Pallas kernels: 81.9 us -> 80.8 us  [per_device(): pl.pallas_call(kernel, out_shape=pltpu.VMEM(density.shape, f32), in_specs...]
where the time goes in v4:
time: 81.7 us; the launch traced here: 81.6 us
  Pallas kernels  80.8 us (99%)
    pallas_call x1, Pallas kernels, per_device(): pl.pallas_call(kernel, out_shape=pltpu.VMEM(density.shape, f32), in_specs...  80.8 us

profile of v4, /device:TPU:1, one launch (start us, length us, event | category | flops | bytes accessed | tf_op | source)
XLA Modules:
  0.0 81.6 jit_solution(3411832745193709517)
XLA Ops:
  0.0 80.8 %polar_steps.1 = f32[128,1024]{1,0:T(8,128)S(1)} custom-call(bf16[128,1024]{1,0:T(8,128)(2,1)} %density.1, s32[32,32]{1,0:T(8,128)} %pattern_in.1), custom_call_target="tpu_custom_call" | custom-call | tf_op jit(solution)/shard_map/polar_steps/pallas_call | solution.py:372
  80.8 0.8 copy.4

commit v5 on v4

--- a/solution.py
+++ b/solution.py
@@ -19,8 +19,9 @@
 
 GROUPS = ("first", "second", "step 1", "step 2", "relay", "relay again")
 STEP_GROUPS = GROUPS[2:4]
-MERGED = ((0, 0), (0, 1), (0, 2), (0, 3))
-ARRIVALS = 66 + len(MERGED)
+PACED = (0,)
+MERGED = ((0,2),(0,3))
+ARRIVALS = 67 + len(MERGED)
 DIRECT = (2, 3)
 
 
@@ -33,7 +34,7 @@
 
 
 def kernel(density, pattern_in, out, loaded, pattern, rows_i, rows_j, send_q, got_q, terms_q, square, send_c, got_c, terms_c, passing, got_f, got_own, turned_rest,
-           unit, relay, turned, load_sem, send_sem, recv_sem):
+           unit, relay, turned, halfway, load_sem, send_sem, recv_sem, pace):
     grid_pos = lax.axis_index("grid")
     y = lax.axis_index("rep")
     x = grid_pos // 8
@@ -135,21 +136,39 @@
         for d, half in ((1, 1), (3, 0)):
             here = place("j", RING - d, half)
             send(here, here, sibling, "first", "shared")
+        pass_half_on(p, q)
         await_copy(total(2 * bytes_of(own[0])), "far", "j")
         for half in range(2):
             here = place("j", 2, half)
             send(here, here, sibling, "first", "shared")
         await_copy(total(4 * bytes_of(own[0])), "late", "i")
-        await_copy(total(6 * bytes_of(own[0])), "shared")
+
+    def await_shared():
+        await_copy(total(6 * HALF * 2 * rows_j.shape[2]), "shared")
 
     def send_unit(step, p, q, cols):
         lag = turn(p - q, RING)
-        at = slot("relay", step)
-
-        @pl.when(lag != 0)
+        at, group = slot("relay", step), GROUPS.index("relay") + step
+
+        @pl.when((lag == 1) | (lag == 3) if step == 0 else lag != 0)
         def _():
-            copy_at(unit.at[step, :, cols], relay.at[step, lag - 1, :, cols], GROUPS.index("relay") + step, at,
-                    device(step, p, p, z, core)).start()
+            copy_at(unit.at[step, :, cols], relay.at[step, lag - 1, :, cols], group, at, device(step, p, p, z, core)).start()
+
+        if step == 0:
+            @pl.when(lag == 2)
+            def _():
+                for b, d in enumerate((1, 3)):
+                    copy_at(unit.at[0, pl.ds(b * BLOCK, BLOCK)], halfway, group, slot("halfway"),
+                            device(0, p, turn(q, d), z, core)).start()
+
+    def pass_half_on(p, q):
+        lag = turn(p - q, RING)
+
+        @pl.when((lag == 1) | (lag == 3))
+        def _():
+            await_copy(halfway, "halfway")
+            copy_at(halfway, relay.at[0, 1, rows((lag // 2) * BLOCK, BLOCK)], GROUPS.index("relay"), slot("relay", 0),
+                    device(0, p, p, z, core)).start()
 
     def pass_units_on(step, p, q):
         at, onward = slot("relay", step), slot("turned", step)
@@ -173,7 +192,12 @@
         def drain(ref):
             copy_at(ref, ref, GROUPS.index("relay") + step, 0, (grid_pos, y)).wait_send()
 
-        pl.when(p != q)(lambda: drain(unit.at[step]))
+        if step == 0:
+            lag = turn(p - q, RING)
+            pl.when(lag == 2)(lambda: drain(unit.at[0]))
+            pl.when((lag == 1) | (lag == 3))(lambda: drain(total(bytes_of(unit.at[0]) + bytes_of(halfway))))
+        else:
+            pl.when(p != q)(lambda: drain(unit.at[step]))
         pl.when(p == q)(lambda: drain(relay.at[step]))
 
     def tile_j(p_at, chunk, core_at):
@@ -214,15 +238,32 @@
         await_copy(total(6 * bytes_of(tile_i(z, 0, core))), "slab again", chunk)
 
     def square_terms(step, p, q):
-        for half in range(2):
-            lines = pl.ds(half * PAIR, PAIR)
-            terms_q[lines, :] = nt_dot(rows_i[step, lines, :], rows_j[step])
-            send_q[step, lines, :] = terms_q[lines, :].astype(jnp.bfloat16)
+        def send_strips(half, first=0, count=PAIR):
             for strip in range(4 * half, 4 * half + 4):
                 part = pl.ds(strip * HALF, HALF)
                 for d in FAR_FIRST:
-                    send(send_q.at[step, part, rows(turn(q, d) * PAIR, PAIR)], got_q.at[step, d - 1, part],
+                    send(send_q.at[step, part, rows(turn(q, d) * PAIR + first, count)],
+                         got_q.at[step, d - 1, part, rows(first, count)],
                          device(step, p, turn(q, d), z, core), STEP_GROUPS[step], "q", step, strip)
+
+        for half in range(2):
+            lines = pl.ds(half * PAIR, PAIR)
+            if (step, half) == (0, 0):
+                for by in (core, other):
+                    right = jnp.concatenate([rows_j[0, rows(t * PAIR + by * BLOCK, BLOCK), :] for t in range(RING)], axis=0)
+                    value = nt_dot(rows_i[0, lines, :], right)
+                    for t in range(RING):
+                        cols = rows(t * PAIR + by * BLOCK, BLOCK)
+                        piece = value[:, t * BLOCK:(t + 1) * BLOCK]
+                        terms_q[lines, cols] = piece
+                        send_q[0, lines, cols] = piece.astype(jnp.bfloat16)
+                    send_strips(0, by * BLOCK, BLOCK)
+                    if by is core:
+                        await_shared()
+                continue
+            terms_q[lines, :] = nt_dot(rows_i[step, lines, :], rows_j[step])
+            send_q[step, lines, :] = terms_q[lines, :].astype(jnp.bfloat16)
+            send_strips(half)
 
     def add_square(step, p, q, strip):
         part = pl.ds(strip * HALF, HALF)
@@ -234,12 +275,16 @@
             scale = keep(block_of(p, strip // 2, core), block_of(q, z, b)) * (1.0 / ORDER)
             square[step, part, rows(z * PAIR + b * BLOCK, BLOCK)] = (
                 terms[:, b * BLOCK:(b + 1) * BLOCK] * scale).astype(jnp.bfloat16)
+        if step in PACED and strip % 2 == 1:
+            pl.semaphore_signal(pace.at[step], inc=1, device_id=device(step, p, q, z, other), device_id_type=MESH)
         block = square.at[step, part, rows(z * PAIR, PAIR)]
         for d in NEAR_FIRST:
             send(block, block, device(step, p, q, turn(z, d), core), STEP_GROUPS[step], "r", step, strip // 2)
 
     def cubic_terms(step, p, q, chunk):
         part = pl.ds(chunk * BLOCK, BLOCK)
+        if step in PACED:
+            pl.semaphore_wait(pace.at[step], 1)
         await_copy(got_q.at[step, :, part], "r", step, chunk)
         for b in range(4):
             lines = pl.ds(b * PAIR, PAIR)
@@ -393,9 +438,11 @@
             pltpu.VMEM((STEPS, PAIR, 4 * BLOCK), bf16),
             pltpu.VMEM((STEPS, 3, PAIR, 4 * BLOCK), bf16),
             pltpu.VMEM((STEPS, PAIR, 4 * BLOCK), bf16),
+            pltpu.VMEM((BLOCK, 4 * BLOCK), bf16),
             pltpu.SemaphoreType.DMA((2,)),
             pltpu.SemaphoreType.DMA((len(GROUPS),)),
             pltpu.SemaphoreType.DMA((ARRIVALS,)),
+            pltpu.SemaphoreType.REGULAR((STEPS,)),
         ],
         compiler_params=pltpu.CompilerParams(
             collective_id=0, has_side_effects=True, vmem_limit_bytes=56 * 2**20

time: 81.7 us -> 80.8 us (0.989)
  Pallas kernels: 80.8 us -> 79.9 us
    pallas_call x1, Pallas kernels: 80.8 us -> 79.9 us  [per_device(): pl.pallas_call(kernel, out_shape=pltpu.VMEM(density.shape, f32), in_specs...]
where the time goes in v5:
time: 80.8 us; the launch traced here: 80.7 us
  Pallas kernels  79.9 us (99%)
    pallas_call x1, Pallas kernels, per_device(): pl.pallas_call(kernel, out_shape=pltpu.VMEM(density.shape, f32), in_specs...  79.9 us

profile of v5, /device:TPU:1, one launch (start us, length us, event | category | flops | bytes accessed | tf_op | source)
XLA Modules:
  0.0 80.7 jit_solution(6003031763800726531)
XLA Ops:
  0.0 79.9 %polar_steps.1 = f32[128,1024]{1,0:T(8,128)S(1)} custom-call(bf16[128,1024]{1,0:T(8,128)(2,1)} %density.1, s32[32,32]{1,0:T(8,128)} %pattern_in.1), custom_call_target="tpu_custom_call" | custom-call | tf_op jit(solution)/shard_map/polar_steps/pallas_call | solution.py:417
  79.9 0.8 copy.4

commit v6 on v5

--- a/solution.py
+++ b/solution.py
@@ -15,7 +15,7 @@
 PAIR = 2 * BLOCK
 HALF = BLOCK // 2
 FAR_FIRST = (2, 1, 3)
-NEAR_FIRST = (1, 3, 2)
+NEAR_FIRST = (2, 1, 3)
 
 GROUPS = ("first", "second", "step 1", "step 2", "relay", "relay again")
 STEP_GROUPS = GROUPS[2:4]

time: 80.8 us -> 79.9 us (0.989)
  Pallas kernels: 79.9 us -> 79 us
    pallas_call x1, Pallas kernels: 79.9 us -> 79 us  [per_device(): pl.pallas_call(kernel, out_shape=pltpu.VMEM(density.shape, f32), in_specs...]
where the time goes in v6:
time: 79.9 us; the launch traced here: 79.8 us
  Pallas kernels  79 us (99%)
  local copies, waits for them, and re-layouts  0.8 us (1%)
    pallas_call x1, Pallas kernels, per_device(): pl.pallas_call(kernel, out_shape=pltpu.VMEM(density.shape, f32), in_specs...  79 us

profile of v6, /device:TPU:1, one launch (start us, length us, event | category | flops | bytes accessed | tf_op | source)
XLA Modules:
  0.0 79.8 jit_solution(16155535563592339846)
XLA Ops:
  0.0 79.0 %polar_steps.1 = f32[128,1024]{1,0:T(8,128)S(1)} custom-call(bf16[128,1024]{1,0:T(8,128)(2,1)} %density.1, s32[32,32]{1,0:T(8,128)} %pattern_in.1), custom_call_target="tpu_custom_call" | custom-call | tf_op jit(solution)/shard_map/polar_steps/pallas_call | solution.py:417
  79.0 0.8 copy.4

commit v7 on v6

--- a/solution.py
+++ b/solution.py
@@ -20,8 +20,7 @@
 GROUPS = ("first", "second", "step 1", "step 2", "relay", "relay again")
 STEP_GROUPS = GROUPS[2:4]
 PACED = (0,)
-MERGED = ((0,2),(0,3))
-ARRIVALS = 67 + len(MERGED)
+ARRIVALS = 67
 DIRECT = (2, 3)
 
 
@@ -33,7 +32,7 @@
     return outer * 8 + z * 2 + core
 
 
-def kernel(density, pattern_in, out, loaded, pattern, rows_i, rows_j, send_q, got_q, terms_q, square, send_c, got_c, terms_c, passing, got_f, got_own, turned_rest,
+def kernel(density, pattern_in, out, loaded, pattern, rows_i, rows_j, got_q, terms_q, square, got_c, terms_c, got_f, got_own, turned_rest,
            unit, relay, turned, halfway, load_sem, send_sem, recv_sem, pace):
     grid_pos = lax.axis_index("grid")
     y = lax.axis_index("rep")
@@ -242,7 +241,7 @@
             for strip in range(4 * half, 4 * half + 4):
                 part = pl.ds(strip * HALF, HALF)
                 for d in FAR_FIRST:
-                    send(send_q.at[step, part, rows(turn(q, d) * PAIR + first, count)],
+                    send(terms_q.at[step, part, rows(turn(q, d) * PAIR + first, count)],
                          got_q.at[step, d - 1, part, rows(first, count)],
                          device(step, p, turn(q, d), z, core), STEP_GROUPS[step], "q", step, strip)
 
@@ -255,22 +254,20 @@
                     for t in range(RING):
                         cols = rows(t * PAIR + by * BLOCK, BLOCK)
                         piece = value[:, t * BLOCK:(t + 1) * BLOCK]
-                        terms_q[lines, cols] = piece
-                        send_q[0, lines, cols] = piece.astype(jnp.bfloat16)
+                        terms_q[step, lines, cols] = piece
                     send_strips(0, by * BLOCK, BLOCK)
                     if by is core:
                         await_shared()
                 continue
-            terms_q[lines, :] = nt_dot(rows_i[step, lines, :], rows_j[step])
-            send_q[step, lines, :] = terms_q[lines, :].astype(jnp.bfloat16)
+            terms_q[step, lines, :] = nt_dot(rows_i[step, lines, :], rows_j[step])
             send_strips(half)
 
     def add_square(step, p, q, strip):
         part = pl.ds(strip * HALF, HALF)
         await_copy(got_q.at[step, :, part], "q", step, strip)
-        terms = terms_q[part, rows(q * PAIR, PAIR)]
+        terms = terms_q[step, part, rows(q * PAIR, PAIR)]
         for d in FAR_FIRST:
-            terms += got_q[step, d - 1, part, :].astype(jnp.float32)
+            terms += got_q[step, d - 1, part, :]
         for b in range(2):
             scale = keep(block_of(p, strip // 2, core), block_of(q, z, b)) * (1.0 / ORDER)
             square[step, part, rows(z * PAIR + b * BLOCK, BLOCK)] = (
@@ -279,55 +276,34 @@
             pl.semaphore_signal(pace.at[step], inc=1, device_id=device(step, p, q, z, other), device_id_type=MESH)
         block = square.at[step, part, rows(z * PAIR, PAIR)]
         for d in NEAR_FIRST:
-            send(block, block, device(step, p, q, turn(z, d), core), STEP_GROUPS[step], "r", step, strip // 2)
+            send(block, block, device(step, p, q, turn(z, d), core), ("step 1", "first")[step], "r", step, strip // 2)
 
     def cubic_terms(step, p, q, chunk):
         part = pl.ds(chunk * BLOCK, BLOCK)
         if step in PACED:
             pl.semaphore_wait(pace.at[step], 1)
-        await_copy(got_q.at[step, :, part], "r", step, chunk)
+        await_copy(total(3 * BLOCK * PAIR * 2), "r", step, chunk)
         for b in range(4):
             lines = pl.ds(b * PAIR, PAIR)
-            terms_c[chunk, lines] = nt_dot(rows_j[step, lines, :], square[step, part, :])
-            send_c[step, chunk, lines] = terms_c[chunk, lines].astype(jnp.bfloat16)
-        if (step, chunk) in MERGED:
-            for b, d in enumerate((1, 3)):
-                send(send_c.at[step, chunk, rows(turn(q, 2) * PAIR + b * BLOCK, BLOCK)], passing.at[chunk, b],
-                     device(step, p, turn(q, d), z, core), STEP_GROUPS[step], "via", step, chunk)
-            for b, d in enumerate((1, 3)):
-                send_cubic(step, p, q, chunk, 1 - b, d)
-        elif step == 0:
+            terms_c[step, chunk, lines] = nt_dot(rows_j[step, lines, :], square[step, part, :])
+        if step == 0:
             for d in FAR_FIRST:
-                send(send_c.at[0, chunk, rows(turn(q, d) * PAIR, PAIR)], got_c.at[d - 1, chunk],
+                send(terms_c.at[0, chunk, rows(turn(q, d) * PAIR, PAIR)], got_c.at[d - 1, chunk],
                      device(0, p, turn(q, d), z, core), STEP_GROUPS[0], "c", 0, chunk)
         else:
             for d in FAR_FIRST:
                 for to in (core, other):
-                    send(send_c.at[1, chunk, rows(turn(q, d) * PAIR + to * BLOCK, BLOCK)], got_f.at[d - 1, chunk, core],
+                    send(terms_c.at[1, chunk, rows(turn(q, d) * PAIR + to * BLOCK, BLOCK)], got_f.at[d - 1, chunk, core],
                          device(1, p, turn(q, d), z, to), STEP_GROUPS[1], "c", 1, chunk)
-            send(terms_c.at[chunk, rows(q * PAIR + other * BLOCK, BLOCK)], got_own.at[chunk], device(1, p, q, z, other),
+            send(terms_c.at[1, chunk, rows(q * PAIR + other * BLOCK, BLOCK)], got_own.at[chunk], device(1, p, q, z, other),
                  STEP_GROUPS[1], "own", chunk)
 
-    def send_cubic(step, p, q, chunk, b, d):
-        send(send_c.at[step, chunk, rows(turn(q, d) * PAIR + b * BLOCK, BLOCK)],
-             got_c.at[d - 1, chunk, pl.ds(b * BLOCK, BLOCK)],
-             device(step, p, turn(q, d), z, core), STEP_GROUPS[step], "c", step, chunk)
-
-    def merge_terms(step, p, q, chunk):
-        if (step, chunk) not in MERGED:
-            return
-        await_copy(passing.at[chunk], "via", step, chunk)
-        for b, d in enumerate((1, 3)):
-            half = rows(turn(q, d) * PAIR + b * BLOCK, BLOCK)
-            send_c[step, chunk, half, :] = (terms_c[chunk, half, :] + passing[chunk, b].astype(jnp.float32)).astype(jnp.bfloat16)
-            send_cubic(step, p, q, chunk, b, d)
-
     def add_cubic(p, q, chunk):
-        sources = (1, 3) if (0, chunk) in MERGED else FAR_FIRST
+        sources = FAR_FIRST
         await_copy(got_c.at[pl.ds(0, len(sources)), chunk], "c", 0, chunk)
-        terms = terms_c[chunk, rows(q * PAIR, PAIR), :]
+        terms = terms_c[0, chunk, rows(q * PAIR, PAIR), :]
         for d in sources:
-            terms += got_c[d - 1, chunk].astype(jnp.float32)
+            terms += got_c[d - 1, chunk]
         cols = pl.ds(chunk * BLOCK, BLOCK)
         updated = 1.5 * turned[0, :, cols].astype(jnp.float32) - 0.5 * terms
         for b in range(2):
@@ -343,14 +319,14 @@
     def put_out(p, q, chunk):
         if chunk == 0:
             await_copy(turned_rest, "turned rest")
-        await_copy(total(6 * bytes_of(got_own.at[0]) // 2), "c", 1, chunk)
+        await_copy(total(6 * bytes_of(got_own.at[0])), "c", 1, chunk)
         await_copy(got_own.at[chunk], "own", chunk)
         cols = pl.ds(chunk * BLOCK, BLOCK)
         mine = rows(core * BLOCK, BLOCK)
-        for by, terms, state in ((core, terms_c[chunk, rows(q * PAIR + core * BLOCK, BLOCK), :], turned[1, mine, cols]),
+        for by, terms, state in ((core, terms_c[1, chunk, rows(q * PAIR + core * BLOCK, BLOCK), :], turned[1, mine, cols]),
                                  (other, got_own[chunk], turned_rest[:, cols])):
             for d in FAR_FIRST:
-                terms += got_f[d - 1, chunk, by].astype(jnp.float32)
+                terms += got_f[d - 1, chunk, by]
             updated = 1.5 * state.astype(jnp.float32) - 0.5 * terms
             out[:, rows((2 * chunk + by) * BLOCK, BLOCK)] = updated * keep(block_of(q, z, core), block_of(p, chunk, by))
 
@@ -379,16 +355,12 @@
         add_square(*at, 6)
         cubic_terms(*at, 1)
         if step == 0:
-            merge_terms(*at, 0)
             add_square(*at, 7)
             cubic_terms(*at, 2)
-            merge_terms(*at, 1)
             await_turned(*at)
             add_cubic(p, q, 0)
             cubic_terms(*at, 3)
-            merge_terms(*at, 2)
             add_cubic(p, q, 1)
-            merge_terms(*at, 3)
             pass_chunk_on(0, q, p)
             add_cubic(p, q, 2)
             pass_chunk_on(1, q, p)
@@ -424,15 +396,12 @@
             pltpu.SMEM(pattern.shape, jnp.int32),
             pltpu.VMEM((STEPS, 4 * BLOCK, quarter), bf16),
             pltpu.VMEM((STEPS, 8 * BLOCK, quarter), bf16),
+            pltpu.VMEM((STEPS, 3, 4 * BLOCK, PAIR), f32),
+            pltpu.VMEM((STEPS, 4 * BLOCK, quarter), f32),
             pltpu.VMEM((STEPS, 4 * BLOCK, quarter), bf16),
-            pltpu.VMEM((STEPS, 3, 4 * BLOCK, PAIR), bf16),
-            pltpu.VMEM((4 * BLOCK, quarter), f32),
-            pltpu.VMEM((STEPS, 4 * BLOCK, quarter), bf16),
-            pltpu.VMEM((STEPS, 4, quarter, BLOCK), bf16),
-            pltpu.VMEM((3, 4, PAIR, BLOCK), bf16),
-            pltpu.VMEM((4, quarter, BLOCK), f32),
-            pltpu.VMEM((4, 2, BLOCK, BLOCK), bf16),
-            pltpu.VMEM((3, 4, 2, BLOCK, BLOCK), bf16),
+            pltpu.VMEM((3, 4, PAIR, BLOCK), f32),
+            pltpu.VMEM((STEPS, 4, quarter, BLOCK), f32),
+            pltpu.VMEM((3, 4, 2, BLOCK, BLOCK), f32),
             pltpu.VMEM((4, BLOCK, BLOCK), f32),
             pltpu.VMEM((BLOCK, 4 * BLOCK), bf16),
             pltpu.VMEM((STEPS, PAIR, 4 * BLOCK), bf16),

time: 79.9 us -> 126 us (1.58)
  Pallas kernels: 79 us -> 125 us
    pallas_call x1, Pallas kernels: 79 us -> 125 us  [per_device(): pl.pallas_call(kernel, out_shape=pltpu.VMEM(density.shape, f32), in_specs...]
where the time goes in v7:
time: 126 us
  Pallas kernels  125 us (99%)
    pallas_call x1, Pallas kernels, per_device(): pl.pallas_call(kernel, out_shape=pltpu.VMEM(density.shape, f32), in_specs...  125 us

profile of v7, /device:TPU:1, one launch (start us, length us, event | category | flops | bytes accessed | tf_op | source)
XLA Modules:
  0.0 126.0 jit_solution(15934939262292511305)
XLA Ops:
  0.0 125.2 %polar_steps.1 = f32[128,1024]{1,0:T(8,128)S(1)} custom-call(bf16[128,1024]{1,0:T(8,128)(2,1)} %density.1, s32[32,32]{1,0:T(8,128)} %pattern_in.1), custom_call_target="tpu_custom_call" | custom-call | tf_op jit(solution)/shard_map/polar_steps/pallas_call | solution.py:389
  125.2 0.8 copy.4

commit v8 on v6

--- a/solution.py
+++ b/solution.py
@@ -19,9 +19,8 @@
 
 GROUPS = ("first", "second", "step 1", "step 2", "relay", "relay again")
 STEP_GROUPS = GROUPS[2:4]
-PACED = (0,)
 MERGED = ((0,2),(0,3))
-ARRIVALS = 67 + len(MERGED)
+ARRIVALS = 61 + len(MERGED)
 DIRECT = (2, 3)
 
 
@@ -34,7 +33,7 @@
 
 
 def kernel(density, pattern_in, out, loaded, pattern, rows_i, rows_j, send_q, got_q, terms_q, square, send_c, got_c, terms_c, passing, got_f, got_own, turned_rest,
-           unit, relay, turned, halfway, load_sem, send_sem, recv_sem, pace):
+           unit, relay, turned, halfway, load_sem, send_sem, recv_sem):
     grid_pos = lax.axis_index("grid")
     y = lax.axis_index("rep")
     x = grid_pos // 8
@@ -212,11 +211,11 @@
             send(own, own, device(1, turn(p, 2), q, z, core), "second", "far", chunk)
         for d in (1, 3):
             send(own, own, device(1, turn(p, d), q, z, core), "second", "near", chunk)
-        send(own, own, device(1, p, q, z, other), "second", "shared again", chunk)
+        send(own, own, device(1, p, q, z, other), "second", "shared again")
         for d in NEAR_FIRST:
             for to in (core, other):
                 src = rows_j.at[1, rows(p * PAIR + to * BLOCK, BLOCK), rows((2 * chunk + core) * BLOCK, BLOCK)]
-                send(src, tile_i(z, chunk, core), device(1, p, q, turn(z, d), to), "second", "slab again", chunk)
+                send(src, tile_i(z, chunk, core), device(1, p, q, turn(z, d), to), "second", "slab again")
         tile_i(z, chunk, core)[...] = rows_j[1, rows(p * PAIR + core * BLOCK, BLOCK), rows((2 * chunk + core) * BLOCK, BLOCK)]
 
     def pass_chunk_on(chunk, p, q):
@@ -225,17 +224,18 @@
             here = tile_j(turn(p, RING - d), chunk, core)
             if chunk not in DIRECT and (chunk % 2 == 0) == (d == 1):
                 send(here, here, device(1, turn(p, d), q, z, core), "second", "far", chunk)
-            send(here, here, device(1, p, q, z, other), "second", "shared again", chunk)
+            send(here, here, device(1, p, q, z, other), "second", "shared again")
 
     def finish_chunk(chunk, p, q):
         here = tile_j(turn(p, 2), chunk, core)
         await_copy(here, "far", chunk)
-        send(here, here, device(1, p, q, z, other), "second", "shared again", chunk)
-
-    def await_chunk(chunk, p, q):
-        await_copy(total(4 * bytes_of(tile_j(p, 0, other))), "shared again", chunk)
-        tile_i(z, chunk, other)[...] = rows_j[1, rows(p * PAIR + core * BLOCK, BLOCK), rows((2 * chunk + other) * BLOCK, BLOCK)]
-        await_copy(total(6 * bytes_of(tile_i(z, 0, core))), "slab again", chunk)
+        send(here, here, device(1, p, q, z, other), "second", "shared again")
+
+    def await_chunks(p, q):
+        await_copy(total(16 * bytes_of(tile_j(p, 0, other))), "shared again")
+        for chunk in range(4):
+            tile_i(z, chunk, other)[...] = rows_j[1, rows(p * PAIR + core * BLOCK, BLOCK), rows((2 * chunk + other) * BLOCK, BLOCK)]
+        await_copy(total(24 * bytes_of(tile_i(z, 0, core))), "slab again")
 
     def square_terms(step, p, q):
         def send_strips(half, first=0, count=PAIR):
@@ -275,16 +275,12 @@
             scale = keep(block_of(p, strip // 2, core), block_of(q, z, b)) * (1.0 / ORDER)
             square[step, part, rows(z * PAIR + b * BLOCK, BLOCK)] = (
                 terms[:, b * BLOCK:(b + 1) * BLOCK] * scale).astype(jnp.bfloat16)
-        if step in PACED and strip % 2 == 1:
-            pl.semaphore_signal(pace.at[step], inc=1, device_id=device(step, p, q, z, other), device_id_type=MESH)
         block = square.at[step, part, rows(z * PAIR, PAIR)]
         for d in NEAR_FIRST:
             send(block, block, device(step, p, q, turn(z, d), core), STEP_GROUPS[step], "r", step, strip // 2)
 
     def cubic_terms(step, p, q, chunk):
         part = pl.ds(chunk * BLOCK, BLOCK)
-        if step in PACED:
-            pl.semaphore_wait(pace.at[step], 1)
         await_copy(got_q.at[step, :, part], "r", step, chunk)
         for b in range(4):
             lines = pl.ds(b * PAIR, PAIR)
@@ -366,8 +362,7 @@
             pass_chunk_on(3, p, q)
             finish_chunk(2, p, q)
             finish_chunk(3, p, q)
-            for chunk in range(4):
-                await_chunk(chunk, p, q)
+            await_chunks(p, q)
             pass_units_on(*at)
         square_terms(*at)
         for strip in range(5):
@@ -442,7 +437,6 @@
             pltpu.SemaphoreType.DMA((2,)),
             pltpu.SemaphoreType.DMA((len(GROUPS),)),
             pltpu.SemaphoreType.DMA((ARRIVALS,)),
-            pltpu.SemaphoreType.REGULAR((STEPS,)),
         ],
         compiler_params=pltpu.CompilerParams(
             collective_id=0, has_side_effects=True, vmem_limit_bytes=56 * 2**20

time: 79.9 us -> 80 us (level)
  no operation moved by 1% of the time
where the time goes in v8:
time: 80 us; the launch traced here: 79.9 us
  Pallas kernels  79.1 us (99%)
  local copies, waits for them, and re-layouts  0.8 us (1%)
    pallas_call x1, Pallas kernels, per_device(): pl.pallas_call(kernel, out_shape=pltpu.VMEM(density.shape, f32), in_specs...  79.1 us

profile of v8, /device:TPU:1, one launch (start us, length us, event | category | flops | bytes accessed | tf_op | source)
XLA Modules:
  0.0 79.9 jit_solution(10389253895448693336)
XLA Ops:
  0.0 79.1 %polar_steps.1 = f32[128,1024]{1,0:T(8,128)S(1)} custom-call(bf16[128,1024]{1,0:T(8,128)(2,1)} %density.1, s32[32,32]{1,0:T(8,128)} %pattern_in.1), custom_call_target="tpu_custom_call" | custom-call | tf_op jit(solution)/shard_map/polar_steps/pallas_call | solution.py:412
  79.1 0.8 copy.4
